TPU v7x, 32 devices: a whole 2x2x4 slice. The times are simulated.
32 devices in a mesh: group: 4 (over z), seq: 4 (over y, core), shard: 2 (over x).
Axes of the slice: x: 2, y: 2, z: 4, core: 2. Of those that a mesh axis runs over, the one named last changes fastest.
Arguments:
- text_rows: bfloat16 [4096, 8, 1280], P(('group', 'seq'), 'shard'), may hold values from -64 to 64
- vis_rows: bfloat16 [128, 8, 1280], P(('group', 'seq', 'shard')), may hold values from -6 to 6
- vis_dest: int32 [128, 1], P(('group', 'seq', 'shard')), may hold values from 0 to 3; in each aligned block of 8 rows (0 to 7, 8 to 15, ...) at most 4 rows name the same one
- segments: int32 [4352], P(('group', 'seq')), may hold values from 0 to 7, never falling along the last dimension, each value on 1 to 1088 neighbouring positions
Outputs:
- attended: bfloat16 [4352, 8, 1024], P(('group', 'seq'), 'shard')
Inputs may be any that keep to these rules, and one draw needn't show every extreme that they name: `vis_dest`: in each aligned block of 8 rows (the visual rows listed by one index of group and seq, in device order), no value is named by more than 4 rows, and this bound is reached. `segments`: ids never fall along the sequence; each document covers 1 to 1088 positions, and one covers exactly 1088.
All inputs are finite; a program needn't handle non-finite values.
Results may differ from a plain program's by a relative error of at most 0.0028.
Values may be sent and summed in bfloat16 or wider, within the bound.
A program may use at most 64 MiB of HBM per device.

v0:
```python
import jax
import jax.numpy as jnp
from jax import lax
from jax.sharding import PartitionSpec as P

GQ = 8
DH = 128
CAP = 4
REACH = 4


def shifted(x, axis, by):
    length = lax.axis_size(axis)
    pairs = [(i, i + by) for i in range(length) if 0 <= i + by < length]
    return lax.ppermute(x, axis, pairs)


def attend_head(queries, key_rows, value_rows, visible, live_query):
    scores = lax.dot_general(
        queries, key_rows, (((1,), (1,)), ((), ())), preferred_element_type=jnp.float32
    ) * DH ** (-0.5)
    scores = jnp.where(visible, scores, -1e30)
    row_max = jnp.max(scores, axis=1, keepdims=True)
    weights = jnp.where(visible, jnp.exp(scores - row_max), 0.0)
    row_total = jnp.where(live_query, jnp.sum(weights, axis=1), 1.0)
    weighted = jnp.dot(weights.astype(jnp.bfloat16), value_rows, preferred_element_type=jnp.float32)
    return (weighted / row_total[:, None]).astype(jnp.bfloat16)


def shards(text_rows, vis_rows, vis_dest, segments):
    seq_count = lax.axis_size("seq")
    groups_here = text_rows.shape[1]
    row_width = text_rows.shape[2]
    text_count = text_rows.shape[0]
    dest_wide = jnp.broadcast_to(vis_dest, (vis_dest.shape[0], vis_rows.shape[1]))
    own_rows, own_dest = (
        lax.all_to_all(vis_rows, "shard", split_axis=1, concat_axis=0, tiled=True),
        lax.all_to_all(dest_wide, "shard", split_axis=1, concat_axis=0, tiled=True),
    )
    block_rows = own_rows.shape[0]
    target = own_dest[:, 0]
    onehot = (target[:, None] == jnp.arange(seq_count, dtype=jnp.int32)[None, :]).astype(jnp.int32)
    before = jnp.cumsum(onehot, axis=0) - onehot
    slot_rank = jnp.sum(before * onehot, axis=1)
    slot_id = target * CAP + slot_rank
    placing = jnp.arange(seq_count * CAP, dtype=jnp.int32)[:, None] == slot_id[None, :]
    packed = jnp.dot(
        placing.astype(jnp.bfloat16),
        own_rows.reshape(block_rows, groups_here * row_width),
        preferred_element_type=jnp.float32,
    ).astype(jnp.bfloat16)
    packed = packed.reshape(seq_count, CAP, groups_here, row_width)
    filled = jnp.sum(placing.astype(jnp.int32), axis=1).reshape(seq_count, CAP)
    arrived, present = (
        lax.all_to_all(packed, "seq", split_axis=0, concat_axis=0, tiled=True),
        lax.all_to_all(filled, "seq", split_axis=0, concat_axis=0, tiled=True),
    )
    local_rows = jnp.concatenate(
        [text_rows, arrived.reshape(seq_count * CAP, groups_here, row_width)], axis=0
    )
    live_rows = jnp.concatenate([jnp.ones((text_count,), jnp.int32), present.reshape(-1)])
    row_count = local_rows.shape[0]
    queries = local_rows[:, :, : GQ * DH]
    keyval = local_rows[:, :, GQ * DH :]
    doc_tag = jnp.where(live_rows > 0, segments + 1, 0)
    earlier = []
    for distance in range(REACH, 0, -1):
        earlier.append(shifted((keyval, doc_tag), ("group", "seq"), distance))
    all_keys = jnp.concatenate([received[0] for received in earlier] + [keyval], axis=0)
    all_tags = jnp.concatenate([received[1] for received in earlier] + [doc_tag], axis=0)
    key_count = all_keys.shape[0]
    key_place = jnp.arange(key_count, dtype=jnp.int32) - REACH * row_count
    row_place = jnp.arange(row_count, dtype=jnp.int32)
    live_query = live_rows > 0
    visible = (
        (key_place[None, :] <= row_place[:, None])
        & (all_tags[None, :] == (segments + 1)[:, None])
        & live_query[:, None]
    )
    head_count = groups_here * GQ
    queries_by_head = (
        queries.reshape(row_count, groups_here, GQ, DH)
        .transpose(1, 2, 0, 3)
        .reshape(head_count, row_count, DH)
    )
    keys_by_group = all_keys.transpose(1, 0, 2)

    def one_head(head_index):
        group_index = head_index // GQ
        key_part = lax.dynamic_index_in_dim(keys_by_group, group_index, 0, keepdims=False)
        query_part = lax.dynamic_index_in_dim(queries_by_head, head_index, 0, keepdims=False)
        return attend_head(query_part, key_part[:, :DH], key_part[:, DH:], visible, live_query)

    heads_out = lax.map(one_head, jnp.arange(head_count, dtype=jnp.int32))
    heads_out = heads_out.reshape(groups_here, GQ, row_count, DH).transpose(2, 0, 1, 3)
    return heads_out.reshape(row_count, groups_here, GQ * DH)


def solution(mesh):
    placed = (
        P(("group", "seq"), "shard", None),
        P(("group", "seq", "shard"), None, None),
        P(("group", "seq", "shard"), None),
        P(("group", "seq")),
    )
    return jax.shard_map(
        shards,
        mesh=mesh,
        in_specs=placed,
        out_specs=P(("group", "seq"), "shard", None),
        check_vma=False,
    )
```

profile of v0, /device:TPU:24, one launch (start us, length us, event | category | flops | bytes accessed | tf_op | source)
XLA Modules:
  0.0 372.7 jit_solution(11664892210811040313)
XLA Ops:
  1.2 3.2 all-to-all-start
  6.0 2.2 all-to-all-done
  8.2 3.3 all-to-all-start.1
  11.9 3.9 %all-to-all-done.1 = bf16[4,8,1280]{2,0,1:T(4,128)(2,1)S(1)} async-done(((bf16[4,8,1280]{2,0,1:T(4,128)(2,1)}), bf16[4,8,1280]{2,0,1:T(4,128)(2,1)S(1)}, u32[]{:S(2)}, u32[]{:S(2)}) %all-to-all-start.1) | async-done | bytes 81952 | tf_op jit(solution)/shard_map/all_to_all | solution.py:37
  16.9 3.3 all-to-all-start.2
  20.3 2.1 copy_dynamic-update-slice_fusion
  22.3 2.9 all-to-all-done.2
  26.7 6.1 %all_to_all.45 = s32[4,1,4]{2,1,0:T(1,128)S(1)} all-to-all(s32[4,1,4]{2,1,0:T(1,128)S(1)} %bitcast.63), channel_id=1, replica_groups=mesh['group'=4,'seq'=4,'shard'=2] {'seq'}, dimensions={0} | all-to-all | bytes 128 | tf_op jit(solution)/shard_map/all_to_all | solution.py:56
  34.1 1.9 collective-permute-start.1
  36.0 1.9 collective-permute-start.2
  39.2 1.9 collective-permute-start.5
  41.2 3.6 collective-permute-done.4
  44.8 23.0 %collective-permute-start.6 = (s32[272]{0:T(512)S(1)}, s32[272]{0:T(512)S(1)}, u32[]{:S(2)}, u32[]{:S(2)}) collective-permute-start(s32[272]{0:T(512)S(1)} %get-tuple-element.164), channel_id=1, source_target_pairs={{0,4},{2,6},{4,8},{6,10},{8,12},{10,14},{12,16},{14,18},{16,20},{1... | collective-permute-start | bytes 3272 | tf_op jit(solution)/shard_map/ppermute | solution.py:15
  67.8 1.9 collective-permute-start.3
  69.8 1.9 collective-permute-start.7
  71.7 8.0 %collective-permute-done.7 = s32[272]{0:T(512)S(1)} collective-permute-done((s32[272]{0:T(512)S(1)}, s32[272]{0:T(512)S(1)}, u32[]{:S(2)}, u32[]{:S(2)}) %collective-permute-start.7) | collective-permute-done | bytes 1120 | tf_op jit(solution)/shard_map/ppermute | solution.py:15
  80.7 1.7 copy.27
  88.4 280.0 %while.14 = (s32[]{:T(128)}, bf16[32,272,128]{2,1,0:T(8,128)(2,1)}, s32[32]{0:T(128)S(1)}, bf16[32,272,128]{2,1,0:T(8,128)(2,1)}, bf16[4,1360,256]{2,1,0:T(8,128...) while((s32[]{:T(128)}, bf16[32,272,128]{2,1,0:T(8,128)(2,1)}, ...), condition=%wide.region_6.7_spmd.clone.clone, body=%wide.region_3.6_spmd.clone.clone.sunk | while | flops 197236736 | bytes 6780314 | solution.py:94
  102.2 1.6 fusion.31
  110.9 1.6 fusion.31
  119.6 1.6 fusion.31
  128.4 1.6 fusion.31
  137.1 1.6 fusion.31
  145.9 1.6 fusion.31
  154.6 1.6 fusion.31
  163.4 1.6 fusion.31
  172.1 1.6 fusion.31
  180.9 1.6 fusion.31
  189.6 1.6 fusion.31
  198.4 1.6 fusion.31
  207.1 1.6 fusion.31
  224.6 1.6 fusion.31
  233.4 1.6 fusion.31
  250.9 1.6 fusion.31
  259.6 1.6 fusion.31
  277.1 1.6 fusion.31
  285.9 1.6 fusion.31
  294.6 1.6 fusion.31
  303.4 1.6 fusion.31
  312.1 1.6 fusion.31
  320.9 1.6 fusion.31
  329.6 1.6 fusion.31
  338.4 1.6 fusion.31
  347.1 1.6 fusion.31
  355.9 1.6 fusion.31
  364.6 1.6 fusion.31
  368.4 2.2 copy.36
  370.6 2.1 reshape.67
  (209 shorter events, 143.8 us)
Async XLA Ops:
  1.2 7.0 %all-to-all-start = ((s32[4,2,4]{0,2,1:T(4,128)}), s32[4,2,4]{0,2,1:T(4,128)S(1)}, u32[]{:S(2)}, u32[]{:S(2)}) async-start(s32[4,2,4]{0,2,1:T(4,128)} %broadcast_in_dim.46), calls=%async_computation | async-start | bytes 8192 | tf_op jit(solution)/shard_map/all_to_all | solution.py:38
  8.2 7.5 %all-to-all-start.1 = ((bf16[4,8,1280]{2,0,1:T(4,128)(2,1)}), bf16[4,8,1280]{2,0,1:T(4,128)(2,1)S(1)}, u32[]{:S(2)}, u32[]{:S(2)}) async-start(bf16[4,8,1280]{2,0,1:T(4,128)(2,1)} %copy.23), calls=%async_computation.1 | async-start | bytes 163840 | tf_op jit(solution)/shard_map/all_to_all | solution.py:37
  16.9 8.3 %all-to-all-start.2 = ((bf16[4,4,4,1280]{3,2,1,0:T(4,128)(2,1)}), bf16[4,4,4,1280]{3,2,1,0:T(4,128)(2,1)S(1)}, u32[]{:S(2)}, u32[]{:S(2)}) async-start(bf16[4,4,4,1280]{3,2,1,0:T(4,128)(2,1)} %reshape.61), calls=%async_computation.2 | async-start | bytes 327680 | tf_op jit(solution)/shard_map/all_to_all | solution.py:55
  20.2 17.7 %copy-start.1 = (s32[272]{0:T(512)S(1)}, s32[272]{0:T(512)}, u32[]{:S(2)}) copy-start(s32[272]{0:T(512)} %param.9) | copy-start | bytes 3268
  25.3 57.1 %collective-permute-start = (bf16[272,4,256]{2,0,1:T(8,128)(2,1)S(1)}, bf16[272,4,256]{2,0,1:T(8,128)(2,1)}, u32[]{:S(2)}, u32[]{:S(2)}) collective-permute-start(bf16[272,4,256]{2,0,1:T(8,128)(2,1)S(1)} %slice.31), channel_id=1, source_target_pairs={{0,8},{2,10},{4,12},{6,14},{8,16},{10,18},{12,20},{14,22},{16,24},... | collective-permute-start | bytes 1671176 | tf_op jit(solution)/shard_map/ppermute | solution.py:15
  34.1 49.4 %collective-permute-start.1 = (bf16[272,4,256]{2,0,1:T(8,128)(2,1)S(1)}, bf16[272,4,256]{2,0,1:T(8,128)(2,1)}, u32[]{:S(2)}, u32[]{:S(2)}) collective-permute-start(bf16[272,4,256]{2,0,1:T(8,128)(2,1)S(1)} %slice.31), channel_id=1, source_target_pairs={{0,6},{2,8},{4,10},{6,12},{8,14},{10,16},{12,18},{14,20},{16,22},{... | collective-permute-start | bytes 1671176 | tf_op jit(solution)/shard_map/ppermute | solution.py:15
  36.0 48.6 %collective-permute-start.2 = (bf16[272,4,256]{2,0,1:T(8,128)(2,1)S(1)}, bf16[272,4,256]{2,0,1:T(8,128)(2,1)}, u32[]{:S(2)}, u32[]{:S(2)}) collective-permute-start(bf16[272,4,256]{2,0,1:T(8,128)(2,1)S(1)} %slice.31), channel_id=1, source_target_pairs={{0,4},{2,6},{4,8},{6,10},{8,12},{10,14},{12,16},{14,18},{16,20},{1... | collective-permute-start | bytes 1671176 | tf_op jit(solution)/shard_map/ppermute | solution.py:15
  37.9 6.8 %collective-permute-start.4 = (s32[272]{0:T(512)S(1)}, s32[272]{0:T(512)S(1)}, u32[]{:S(2)}, u32[]{:S(2)}) collective-permute-start(s32[272]{0:T(512)S(1)} %get-tuple-element.164), channel_id=1, source_target_pairs={{0,8},{2,10},{4,12},{6,14},{8,16},{10,18},{12,20},{14,22},{16,24},... | collective-permute-start | bytes 3272 | tf_op jit(solution)/shard_map/ppermute | solution.py:15
  39.2 28.6 %collective-permute-start.5 = (s32[272]{0:T(512)S(1)}, s32[272]{0:T(512)S(1)}, u32[]{:S(2)}, u32[]{:S(2)}) collective-permute-start(s32[272]{0:T(512)S(1)} %get-tuple-element.164), channel_id=1, source_target_pairs={{0,6},{2,8},{4,10},{6,12},{8,14},{10,16},{12,18},{14,20},{16,22},{... | collective-permute-start | bytes 3272 | tf_op jit(solution)/shard_map/ppermute | solution.py:15
  44.8 25.0 %collective-permute-start.6 = (s32[272]{0:T(512)S(1)}, s32[272]{0:T(512)S(1)}, u32[]{:S(2)}, u32[]{:S(2)}) collective-permute-start(s32[272]{0:T(512)S(1)} %get-tuple-element.164), channel_id=1, source_target_pairs={{0,4},{2,6},{4,8},{6,10},{8,12},{10,14},{12,16},{14,18},{16,20},{1... | collective-permute-start | bytes 3272 | tf_op jit(solution)/shard_map/ppermute | solution.py:15
  67.8 17.9 %collective-permute-start.3 = (bf16[272,4,256]{2,0,1:T(8,128)(2,1)S(1)}, bf16[272,4,256]{2,0,1:T(8,128)(2,1)}, u32[]{:S(2)}, u32[]{:S(2)}) collective-permute-start(bf16[272,4,256]{2,0,1:T(8,128)(2,1)S(1)} %slice.31), channel_id=1, source_target_pairs={{0,2},{2,4},{4,6},{6,8},{8,10},{10,12},{12,14},{14,16},{16,18},{18... | collective-permute-start | bytes 1671176 | tf_op jit(solution)/shard_map/ppermute | solution.py:15
  69.8 9.9 %collective-permute-start.7 = (s32[272]{0:T(512)S(1)}, s32[272]{0:T(512)S(1)}, u32[]{:S(2)}, u32[]{:S(2)}) collective-permute-start(s32[272]{0:T(512)S(1)} %get-tuple-element.164), channel_id=1, source_target_pairs={{0,2},{2,4},{4,6},{6,8},{8,10},{10,12},{12,14},{14,16},{16,18},{18... | collective-permute-start | bytes 3272 | tf_op jit(solution)/shard_map/ppermute | solution.py:15
  86.8 1.6 copy-start
where the time goes:
time: 378 us; the launch traced here: 373 us
  loops' own time  106 us (28%)
  matrix products  95.6 us (25%)
  local copies, waits for them, and re-layouts  74 us (20%)
  starting transfers between devices  45 us (12%)
  other arithmetic  25.1 us (7%)
  waiting for transfers between devices  20.5 us (5%)
  blocking collectives  6.08 us (2%)
    another operation x1, loops' own time, shards(): heads_out = lax.map(one_head, jnp.arange(head_count, dtype=jnp.int32))  106 us
    dot_general x32, matrix products, attend_head(): lax.dot_general(queries, key_rows, (((1,), (1,)), ((), ())), preferred_el...  52 us
    dot_general x32, matrix products, attend_head(): jnp.dot(weights.astype(jnp.bfloat16), value_rows, preferred_element_type=...  43.3 us
    squeeze x32, local copies, waits for them, and re-layouts, one_head(): lax.dynamic_index_in_dim(keys_by_group, group_index, 0, keepdims=False)  36.9 us
    ppermute x8, starting transfers between devices, shifted(): return lax.ppermute(x, axis, pairs)  35.2 us
    reduce_sum x32, other arithmetic, attend_head(): row_total = jnp.where(live_query, jnp.sum(weights, axis=1), 1.0)  23.9 us
    dynamic_slice x32, local copies, waits for them, and re-layouts, shards(): heads_out = lax.map(one_head, jnp.arange(head_count, dtype=jnp.int32))  17.7 us
    ppermute x8, waiting for transfers between devices, shifted(): return lax.ppermute(x, axis, pairs)  11.6 us
  transfers between devices with their start and end apart: 11, of which 5 were waited for; matrix products, arithmetic and copies ran while one was open for 3% of the time, Pallas kernels for 0%

commit v1 on v0

v1 whole, which is shorter than its diff:
```python
import functools
import math

import jax
import jax.numpy as jnp
import numpy as np
from jax import lax
from jax.experimental import pallas as pl
from jax.experimental.pallas import tpu as pltpu
from jax.sharding import PartitionSpec as P

GQ = 8
DH = 128
CAP = 4
REACH = 4
FAR = -1e30
LOG2E = math.log2(math.e)
MESH = pl.DeviceIdType.MESH


def up(value, step):
    return -(-value // step) * step


def kernel(
    n_group, n_seq, n_shard, text_ref, vis_ref, seg_row_ref, seg_col_ref, same_ref, pick_ref, slot_ref,
    out_ref, kv_buf, aux_buf, vis_buf, key_all, val_all, bias, slots, live_col,
    send_sem, recv_sem, vis_send, vis_recv,
):
    groups, text, width = text_ref.shape
    query_width = GQ * DH
    rows = out_ref.shape[1]
    slot_count = rows - text
    half = text // 2
    pad = key_all.shape[0] - (REACH + 1) * text
    slot_start = REACH * text + half
    vis_block = vis_ref.shape[1]
    n_source = n_seq * n_shard
    blocks = n_group * n_seq
    aux_rows = groups * slot_count

    my_group, my_seq, my_shard = lax.axis_index("group"), lax.axis_index("seq"), lax.axis_index("shard")
    here = my_group * n_seq + my_seq
    odd = lax.rem(here, 2)
    upper = lax.rem(here // 2, 2)
    sibling = here + 1 - 2 * odd
    partner = here + 2 - 4 * upper
    me = my_seq * n_shard + my_shard

    def device(block):
        return (block // n_seq, lax.rem(block, n_seq), my_shard)

    def peer(index):
        return (my_group, index // n_shard, lax.rem(index, n_shard))

    barrier = pltpu.get_barrier_semaphore()

    def greet(step, carry):
        pl.semaphore_signal(barrier, inc=1, device_id=peer(lax.rem(me + step, n_source)), device_id_type=MESH)
        return carry

    lax.fori_loop(1, n_source, greet, 0)
    pl.semaphore_signal(barrier, inc=1, device_id=device(sibling), device_id_type=MESH)
    pl.semaphore_signal(barrier, inc=1, device_id=device(partner), device_id_type=MESH)

    @pl.when(here >= REACH)
    def _():
        pl.semaphore_signal(barrier, inc=1, device_id=device(here - REACH), device_id_type=MESH)

    for place in range(REACH):
        @pl.when(here < REACH - place)
        def _():
            kv_buf[:, place] = jnp.zeros_like(kv_buf[:, place])
            aux_buf[place] = jnp.zeros_like(aux_buf[place])

    pl.semaphore_wait(barrier, n_source + 1 + (here + REACH < blocks).astype(jnp.int32))

    def landing(item, place):
        return aux_buf.at[place] if item == groups else kv_buf.at[item, place]

    def source(item, place):
        if place < REACH:
            return landing(item, place)
        if item == groups:
            return aux_buf.at[REACH]
        return text_ref.at[item, :, pl.ds(query_width, 2 * DH)]

    def transfer(item, number, place, target_place, target):
        return pltpu.make_async_remote_copy(
            src_ref=source(item, place),
            dst_ref=landing(item, target_place),
            send_sem=send_sem.at[item, number],
            recv_sem=recv_sem.at[item, target_place],
            device_id=device(target),
            device_id_type=MESH,
        )

    own_copies = [
        (here + REACH < blocks, 0, 4, 0, here + REACH),
        (upper == 0, 1, 4, 2, here + 2),
        (odd == 0, 2, 4, 3, here + 1),
    ]
    far_copies = [
        ((here >= 4) & (upper == 1), 3, 0, 2, here - 2),
        ((here >= 4) & (odd == 1), 4, 0, 1, here - 1),
    ]
    near_copies = [
        ((here >= 2) & (odd == 0), 5, 2, 1, here + 1),
        ((here >= 2) & (odd == 1), 5, 2, 3, here - 1),
    ]

    def start(item, copies):
        for condition, number, place, target_place, target in copies:
            @pl.when(condition)
            def _():
                transfer(item, number, place, target_place, target).start()

    def finish(item, copies):
        for condition, number, place, target_place, target in copies:
            @pl.when(condition)
            def _():
                transfer(item, number, place, target_place, target).wait_send()

    def arrive(item, place):
        @pl.when(here >= REACH - place)
        def _():
            transfer(item, 0, place, place, sibling).wait_recv()

    def relay_far(item):
        arrive(item, 0)
        start(item, far_copies)

    def relay_near(item):
        arrive(item, 2)
        start(item, near_copies)

    def vis_copy(step, landing_index):
        target = lax.rem(me + step, n_source)
        return pltpu.make_async_remote_copy(
            src_ref=vis_ref.at[lax.rem(target, n_shard)],
            dst_ref=vis_buf.at[landing_index],
            send_sem=vis_send.at[step],
            recv_sem=vis_recv.at[step],
            device_id=peer(target),
            device_id_type=MESH,
        )

    def vis_start(step, carry):
        vis_copy(step, me).start()
        return carry

    lax.fori_loop(1, n_source, vis_start, 0)
    for item in range(groups):
        start(item, own_copies)
    vis_buf[me] = vis_ref[my_shard]

    def vis_wait(step, carry):
        vis_copy(step, lax.rem(me + n_source - step, n_source)).wait_recv()
        return carry

    lax.fori_loop(1, n_source, vis_wait, 0)

    block_rows = n_shard * vis_block
    my_dest = my_seq.astype(jnp.float32)
    filled = jnp.zeros((aux_rows, 1), jnp.float32)
    for seq in range(n_seq):
        listed = vis_buf[seq * n_shard:(seq + 1) * n_shard].reshape(block_rows, width + DH)
        dest = listed[:, width:].astype(jnp.float32)
        dest_across = dest.T[0:1, :]
        earlier = jnp.where(dest[:, 0:1] == dest_across, same_ref[...], 0.0)
        rank = jnp.sum(earlier, axis=0, keepdims=True)
        placing = jnp.where(
            (slot_ref[...] == rank + float(seq * CAP)) & (dest_across == my_dest), pick_ref[...], 0.0
        )
        part = jnp.dot(placing.astype(jnp.bfloat16), listed[:, :width], preferred_element_type=jnp.float32)
        slots[...] = part if seq == 0 else slots[...] + part
        filled = filled + jnp.sum(placing, axis=1, keepdims=True)
    aux_buf[REACH, 0:aux_rows] = slots[:, query_width:].astype(jnp.bfloat16)
    live_col[...] = jnp.broadcast_to(filled[:slot_count], live_col.shape)
    live_across = live_col[...].T[0:1, :]
    seg_row = seg_row_ref[...].astype(jnp.float32) + 1.0
    text_tags = seg_row[:, :text]
    slot_tags = jnp.where(live_across > 0, seg_row[:, text:], 0.0)
    tag_rows = jnp.concatenate(
        [
            jnp.broadcast_to(text_tags, (8, text)),
            jnp.concatenate(
                [jnp.broadcast_to(slot_tags, (8, slot_count)), jnp.zeros((8, text - slot_count), jnp.float32)], axis=1
            ),
        ],
        axis=0,
    )
    aux_buf[REACH, aux_rows:] = tag_rows.astype(jnp.bfloat16)
    start(groups, own_copies)

    relay_far(0)
    relay_far(groups)
    relay_near(0)
    relay_near(groups)
    if groups > 1:
        relay_far(1)
    arrive(groups, 1)
    arrive(groups, 3)

    all_tags, all_places = [], []

    def lane_places(count):
        return lax.broadcasted_iota(jnp.int32, (1, count), 1)

    for place in range(REACH):
        all_tags.append(aux_buf[place, aux_rows:].astype(jnp.float32)[0:1, :])
        all_places.append(lane_places(text) - (REACH - place) * rows)
    slot_tag_list, slot_place_list = [], []
    for place in range(REACH + 1):
        slot_tag_list.append(aux_buf[place, aux_rows:].astype(jnp.float32)[8:9, :slot_count])
        slot_place_list.append(lane_places(slot_count) - (REACH - place) * rows + text)
    spare = pad - (REACH + 1) * slot_count
    if spare:
        slot_tag_list.append(jnp.zeros((1, spare), jnp.float32))
        slot_place_list.append(jnp.zeros((1, spare), jnp.int32))
    all_tags += [text_tags[:, :half]] + slot_tag_list + [text_tags[:, half:]]
    all_places += [lane_places(half)] + slot_place_list + [lane_places(half) + half]
    tags = jnp.concatenate(all_tags, axis=1)
    places = jnp.concatenate(all_places, axis=1)
    row_tags = seg_col_ref[...].astype(jnp.float32) + 1.0
    row_places = lax.broadcasted_iota(jnp.int32, (rows, 1), 0)
    for first in range(0, rows, 16):
        part = slice(first, first + 16)
        seen = (tags == row_tags[part]) & (places <= row_places[part])
        bias[part, :] = jnp.where(seen, 0.0, FAR)

    val_all[:, DH:] = jnp.ones_like(val_all[:, DH:])
    if spare:
        blank = jnp.zeros((spare, DH), jnp.bfloat16)
        key_all[slot_start + pad - spare:slot_start + pad, :] = blank
        val_all[slot_start + pad - spare:slot_start + pad, :DH] = blank
    scale = LOG2E * DH ** -0.5
    total = key_all.shape[0]

    def attend(queries, heads, rows_from, rows_to, low, high):
        count = rows_to - rows_from
        scores = lax.dot_general(
            queries, key_all[low:high], (((1,), (1,)), ((), ())), preferred_element_type=jnp.float32
        )
        scores = (scores.reshape(heads, count, high - low) + bias[rows_from:rows_to, low:high][None]).reshape(
            heads * count, high - low
        )
        largest = jnp.max(scores, axis=1, keepdims=True)
        weights = jnp.exp2((scores - largest) * scale).astype(jnp.bfloat16)
        summed = jnp.dot(weights, val_all[low:high], preferred_element_type=jnp.float32)
        return summed[:, :DH] / summed[:, DH:]

    together = 2
    for group in range(groups):
        arrive(group, 1)
        arrive(group, 3)
        for place in range(REACH):
            key_all[place * text:(place + 1) * text, :] = kv_buf[group, place, :, :DH]
            val_all[place * text:(place + 1) * text, :DH] = kv_buf[group, place, :, DH:]
        own = text_ref[group, :, query_width:]
        key_all[REACH * text:slot_start, :] = own[:half, :DH]
        val_all[REACH * text:slot_start, :DH] = own[:half, DH:]
        key_all[slot_start + pad:, :] = own[half:, :DH]
        val_all[slot_start + pad:, :DH] = own[half:, DH:]
        for place in range(REACH + 1):
            slot_rows = aux_buf[place, group * slot_count:(group + 1) * slot_count]
            at = slot_start + place * slot_count
            key_all[at:at + slot_count, :] = slot_rows[:, :DH]
            val_all[at:at + slot_count, :DH] = slot_rows[:, DH:]

        def some_heads(index, carry):
            lanes = [pl.ds(pl.multiple_of((index * together + k) * DH, DH), DH) for k in range(together)]
            for rows_from, low, high in ((0, 0, slot_start + pad), (half, half, total)):
                queries = jnp.concatenate(
                    [text_ref[group, rows_from:rows_from + half, lane] for lane in lanes], axis=0
                )
                result = attend(queries, together, rows_from, rows_from + half, low, high).astype(jnp.bfloat16)
                for k, lane in enumerate(lanes):
                    out_ref[group, rows_from:rows_from + half, lane] = result[k * half:(k + 1) * half]
            return carry

        steps = GQ // together
        lax.fori_loop(0, steps // 2, some_heads, 0)
        if group + 1 < groups:
            relay_near(group + 1)
            if group + 2 < groups:
                relay_far(group + 2)
        lax.fori_loop(steps // 2, steps, some_heads, 0)
        slot_queries = slots[group * slot_count:(group + 1) * slot_count, :query_width].astype(jnp.bfloat16)
        queries = jnp.concatenate([slot_queries[:, k * DH:(k + 1) * DH] for k in range(GQ)], axis=0)
        result = attend(queries, GQ, text, rows, text, total)
        live = live_col[...]
        for k in range(GQ):
            head = jnp.where(live > 0, result[k * slot_count:(k + 1) * slot_count], 0.0)
            out_ref[group, text:, k * DH:(k + 1) * DH] = head.astype(jnp.bfloat16)

    for item in range(groups + 1):
        finish(item, own_copies + far_copies + near_copies)

    def vis_finish(step, carry):
        vis_copy(step, me).wait_send()
        return carry

    lax.fori_loop(1, n_source, vis_finish, 0)


def shards(mesh_shape, text_rows, vis_rows, vis_dest, segments):
    n_group, n_seq, n_shard = (mesh_shape[axis] for axis in ("group", "seq", "shard"))
    text, groups, width = text_rows.shape
    rows = segments.shape[0]
    slot_count = n_seq * CAP
    vis_count = vis_rows.shape[0]
    vis_block = up(vis_count * groups, 16)
    text_t = text_rows.transpose(1, 0, 2)
    listed = jnp.concatenate(
        [
            vis_rows,
            jnp.broadcast_to(vis_dest[:, :, None].astype(jnp.bfloat16), (vis_count, vis_rows.shape[1], DH)),
        ],
        axis=2,
    )
    listed = listed.reshape(vis_count, n_shard, groups, width + DH).transpose(1, 0, 2, 3)
    listed = listed.reshape(n_shard, vis_count * groups, width + DH)
    listed = jnp.pad(listed, ((0, 0), (0, vis_block - vis_count * groups), (0, 0)))

    index = np.arange(n_shard * vis_block)
    within = index % vis_block
    valid = within < vis_count * groups
    head = within % groups
    same = (head[:, None] == head[None, :]) & (index[:, None] < index[None, :]) & valid[:, None] & valid[None, :]
    place = np.arange(groups * slot_count)
    pick = (place[:, None] // slot_count == head[None, :]) & valid[None, :]
    slot = np.broadcast_to((place % slot_count)[:, None], pick.shape)

    pad = up((REACH + 1) * slot_count, 128)
    keys = (REACH + 1) * text + pad
    aux_rows = groups * slot_count + 16
    n_source = n_seq * n_shard
    vmem = pl.BlockSpec(memory_space=pltpu.VMEM)
    result = pl.pallas_call(
        functools.partial(kernel, n_group, n_seq, n_shard),
        out_shape=jax.ShapeDtypeStruct((groups, rows, GQ * DH), jnp.bfloat16),
        in_specs=[vmem] * 7,
        out_specs=vmem,
        scratch_shapes=[
            pltpu.VMEM((groups, REACH, text, 2 * DH), jnp.bfloat16),
            pltpu.VMEM((REACH + 1, aux_rows, 2 * DH), jnp.bfloat16),
            pltpu.VMEM((n_source, vis_block, width + DH), jnp.bfloat16),
            pltpu.VMEM((keys, DH), jnp.bfloat16),
            pltpu.VMEM((keys, 2 * DH), jnp.bfloat16),
            pltpu.VMEM((rows, keys), jnp.float32),
            pltpu.VMEM((groups * slot_count, width), jnp.float32),
            pltpu.VMEM((slot_count, DH), jnp.float32),
            pltpu.SemaphoreType.DMA((groups + 1, 6)),
            pltpu.SemaphoreType.DMA((groups + 1, REACH)),
            pltpu.SemaphoreType.DMA((n_source,)),
            pltpu.SemaphoreType.DMA((n_source,)),
        ],
        compiler_params=pltpu.CompilerParams(
            collective_id=0, has_side_effects=True, vmem_limit_bytes=56 * 1024 * 1024
        ),
    )(
        text_t,
        listed,
        segments[None, :],
        segments[:, None],
        jnp.asarray(same, jnp.float32),
        jnp.asarray(pick, jnp.float32),
        jnp.asarray(slot, jnp.float32),
    )
    return result.transpose(1, 0, 2)


def solution(mesh):
    placed = (
        P(("group", "seq"), "shard", None),
        P(("group", "seq", "shard"), None, None),
        P(("group", "seq", "shard"), None),
        P(("group", "seq")),
    )
    return jax.shard_map(
        functools.partial(shards, dict(mesh.shape)),
        mesh=mesh,
        in_specs=placed,
        out_specs=P(("group", "seq"), "shard", None),
        check_vma=False,
    )
```

time: 378 us -> 65.4 us (0.17)
  the two profiles are of different devices: /device:TPU:24 before, /device:TPU:9 now
where the time goes in v1:
time: 65.4 us; the launch traced here: 64.8 us
  Pallas kernels  51.5 us (79%)
  local copies, waits for them, and re-layouts  11.7 us (18%)
  other arithmetic  1.55 us (2%)
    pallas_call x1, Pallas kernels, shards(): pl.pallas_call(functools.partial(kernel, n_group, n_seq, n_shard), out_sh...  51.5 us
    transpose x1, local copies, waits for them, and re-layouts, shards(): return result.transpose(1, 0, 2)  4.71 us
    unnamed x1, local copies, waits for them, and re-layouts  3.56 us
    broadcast_in_dim x1, local copies, waits for them, and re-layouts, shards(): segments[:, None]  1.44 us

profile of v1, /device:TPU:9, one launch (start us, length us, event | category | flops | bytes accessed | tf_op | source)
XLA Modules:
  0.0 64.8 jit_solution(16947505273428774860)
XLA Ops:
  0.0 0.7 %convert_bitcast_fusion = bf16[4]{0:T(256)(128)(2,1)S(1)} fusion(s32[4,1]{0,1:T(1,128)} %param.9), kind=kLoop, calls=%fused_computation.3 | loop fusion | flops 4 | bytes 24 | tf_op jit(solution)/shard_map/convert_element_type | solution.py:318
  0.7 1.2 %broadcast_in_dim.13.seg_row_ref = s32[1,272]{1,0:T(1,128)} reshape(s32[272]{0:T(512)} %param.10) | data formatting | bytes 2176 | tf_op jit(solution)/shard_map/broadcast_in_dim | solution.py:365
  1.9 0.1 broadcast_in_dim.12
  2.0 0.9 %pad_maximum_fusion = bf16[4,8,1408]{2,1,0:T(8,128)(2,1)S(1)} fusion(bf16[4,8,128]{2,1,0:T(8,128)(2,1)S(1)} %broadcast_in_dim.12, bf16[4,8,1280]{2,1,0:T(8,128)(2,1)} %param.8), kind=kLoop, calls=%fused_computation.1 | loop fusion | flops 180224 | bytes 180224 | tf_op jit(solution)/shard_map/concatenate | solution.py:315
  2.9 0.7 %reshape.15.vis_ref = bf16[2,16,1408]{2,1,0:T(8,128)(2,1)} reshape(bf16[2,4,4,1408]{3,2,1,0:T(4,128)(2,1)S(1)} %bitcast.11) | data formatting | bytes 180224 | tf_op jit(solution)/shard_map/reshape | solution.py:323
  3.6 1.4 %broadcast_in_dim.15.seg_col_ref = s32[272,1]{1,0:T(8,128)} reshape(s32[272]{0:T(512)} %param.10) | data formatting | bytes 2176 | tf_op jit(solution)/shard_map/broadcast_in_dim | solution.py:366
  5.0 3.6 %copy.17 = bf16[256,4,1280]{2,0,1:T(8,128)(2,1)} copy(bf16[256,4,1280]{2,1,0:T(4,128)(2,1)} %param.7) | data formatting | bytes 5242880 | tf_op args[0]
  8.6 51.5 %shard_map.73 = bf16[4,272,1024]{2,1,0:T(8,128)(2,1)} custom-call(bf16[4,256,1280]{2,1,0:T(8,128)(2,1)} %bitcast.9, bf16[2,16,1408]{2,1,0:T(8,128)(2,1)} %reshape.15.vis_ref, s32[1,272]{1,0:T(1,128)} %broadcast_in_dim.13.seg_row_ref, s32[272,1]{1,0:T(8,128)} %broadcast_in_dim.15.seg_col_ref, f32[32,32]{1,0:T(8,128)} %constant.3.clone.same_ref, ...), custom_call_target="tpu_custom_call" | custom-call | tf_op jit(solution)/shard_map/pallas_call | solution.py:340
  60.0 4.7 %copy.14 = bf16[272,4,1024]{2,1,0:T(4,128)(2,1)} copy(bf16[272,4,1024]{2,0,1:T(8,128)(2,1)} %bitcast.10) | data formatting | bytes 4456448 | tf_op jit(solution)/shard_map/transpose | solution.py:371
  (2 shorter events, 0.1 us)

commit v2 on v1

--- a/solution.py
+++ b/solution.py
@@ -13,7 +13,8 @@
 DH = 128
 CAP = 4
 REACH = 4
-FAR = -1e30
+FAR = -(2.0 ** 100)
+OWN = 120
 LOG2E = math.log2(math.e)
 MESH = pl.DeviceIdType.MESH
 
@@ -23,8 +24,8 @@
 
 
 def kernel(
-    n_group, n_seq, n_shard, text_ref, vis_ref, seg_row_ref, seg_col_ref, same_ref, pick_ref, slot_ref,
-    out_ref, kv_buf, aux_buf, vis_buf, key_all, val_all, bias, slots, live_col,
+    n_group, n_seq, n_shard, text_ref, vis_ref, dest_ref, seg_ref, same_ref, pick_ref, slot_ref,
+    slot_order_ref, out_ref, kv_buf, aux_buf, vis_stage, vis_buf, key_all, val_all, query_mask, diagonal, slots, live_col,
     send_sem, recv_sem, vis_send, vis_recv,
 ):
     groups, text, width = text_ref.shape
@@ -34,7 +35,7 @@
     half = text // 2
     pad = key_all.shape[0] - (REACH + 1) * text
     slot_start = REACH * text + half
-    vis_block = vis_ref.shape[1]
+    vis_count, vis_block = vis_ref.shape[0], vis_stage.shape[1]
     n_source = n_seq * n_shard
     blocks = n_group * n_seq
     aux_rows = groups * slot_count
@@ -54,6 +55,17 @@
         return (my_group, index // n_shard, lax.rem(index, n_shard))
 
     barrier = pltpu.get_barrier_semaphore()
+
+    vis_wide = vis_ref[...].astype(jnp.float32)
+    dest_wide = dest_ref[...].astype(jnp.float32)
+    for shard in range(n_shard):
+        listed = [vis_wide[row, shard * groups:(shard + 1) * groups] for row in range(vis_count)]
+        names = [jnp.broadcast_to(dest_wide[row:row + 1], (groups, DH)) for row in range(vis_count)]
+        if vis_block > vis_count * groups:
+            listed.append(jnp.zeros((vis_block - vis_count * groups, width), jnp.float32))
+            names.append(jnp.zeros((vis_block - vis_count * groups, DH), jnp.float32))
+        vis_stage[shard, :, :width] = jnp.concatenate(listed, axis=0).astype(jnp.bfloat16)
+        vis_stage[shard, :, width:] = jnp.concatenate(names, axis=0).astype(jnp.bfloat16)
 
     def greet(step, carry):
         pl.semaphore_signal(barrier, inc=1, device_id=peer(lax.rem(me + step, n_source)), device_id_type=MESH)
@@ -137,7 +149,7 @@
     def vis_copy(step, landing_index):
         target = lax.rem(me + step, n_source)
         return pltpu.make_async_remote_copy(
-            src_ref=vis_ref.at[lax.rem(target, n_shard)],
+            src_ref=vis_stage.at[lax.rem(target, n_shard)],
             dst_ref=vis_buf.at[landing_index],
             send_sem=vis_send.at[step],
             recv_sem=vis_recv.at[step],
@@ -152,7 +164,7 @@
     lax.fori_loop(1, n_source, vis_start, 0)
     for item in range(groups):
         start(item, own_copies)
-    vis_buf[me] = vis_ref[my_shard]
+    vis_buf[me] = vis_stage[my_shard]
 
     def vis_wait(step, carry):
         vis_copy(step, lax.rem(me + n_source - step, n_source)).wait_recv()
@@ -178,7 +190,7 @@
     aux_buf[REACH, 0:aux_rows] = slots[:, query_width:].astype(jnp.bfloat16)
     live_col[...] = jnp.broadcast_to(filled[:slot_count], live_col.shape)
     live_across = live_col[...].T[0:1, :]
-    seg_row = seg_row_ref[...].astype(jnp.float32) + 1.0
+    seg_row = seg_ref[...].reshape(1, rows).astype(jnp.float32) + 1.0
     text_tags = seg_row[:, :text]
     slot_tags = jnp.where(live_across > 0, seg_row[:, text:], 0.0)
     tag_rows = jnp.concatenate(
@@ -202,81 +214,90 @@
     arrive(groups, 1)
     arrive(groups, 3)
 
-    all_tags, all_places = [], []
-
-    def lane_places(count):
-        return lax.broadcasted_iota(jnp.int32, (1, count), 1)
-
-    for place in range(REACH):
-        all_tags.append(aux_buf[place, aux_rows:].astype(jnp.float32)[0:1, :])
-        all_places.append(lane_places(text) - (REACH - place) * rows)
-    slot_tag_list, slot_place_list = [], []
+    total = key_all.shape[0]
+    spare = pad - (REACH + 1) * slot_count
+    all_tags = [aux_buf[place, aux_rows:].astype(jnp.float32)[0:1, :] for place in range(REACH)]
+    all_tags.append(text_tags[:, :half])
     for place in range(REACH + 1):
-        slot_tag_list.append(aux_buf[place, aux_rows:].astype(jnp.float32)[8:9, :slot_count])
-        slot_place_list.append(lane_places(slot_count) - (REACH - place) * rows + text)
-    spare = pad - (REACH + 1) * slot_count
+        all_tags.append(aux_buf[place, aux_rows:].astype(jnp.float32)[8:9, :slot_count])
     if spare:
-        slot_tag_list.append(jnp.zeros((1, spare), jnp.float32))
-        slot_place_list.append(jnp.zeros((1, spare), jnp.int32))
-    all_tags += [text_tags[:, :half]] + slot_tag_list + [text_tags[:, half:]]
-    all_places += [lane_places(half)] + slot_place_list + [lane_places(half) + half]
+        all_tags.append(jnp.zeros((1, spare), jnp.float32))
+    all_tags.append(text_tags[:, half:])
     tags = jnp.concatenate(all_tags, axis=1)
-    places = jnp.concatenate(all_places, axis=1)
-    row_tags = seg_col_ref[...].astype(jnp.float32) + 1.0
-    row_places = lax.broadcasted_iota(jnp.int32, (rows, 1), 0)
-    for first in range(0, rows, 16):
-        part = slice(first, first + 16)
-        seen = (tags == row_tags[part]) & (places <= row_places[part])
-        bias[part, :] = jnp.where(seen, 0.0, FAR)
-
-    val_all[:, DH:] = jnp.ones_like(val_all[:, DH:])
-    if spare:
-        blank = jnp.zeros((spare, DH), jnp.bfloat16)
-        key_all[slot_start + pad - spare:slot_start + pad, :] = blank
-        val_all[slot_start + pad - spare:slot_start + pad, :DH] = blank
+    name = lax.broadcasted_iota(jnp.int32, (DH, total), 0)
+    at = lax.broadcasted_iota(jnp.int32, (DH, total), 1) - (slot_start + REACH * slot_count)
+    differs = (name < OWN) & (name.astype(jnp.float32) + 1.0 != tags)
+    own_slot = (name == OWN) & (at >= 0) & (at < slot_count)
+    key_all[:, DH:] = jnp.where(differs | own_slot, FAR, 0.0).T.astype(jnp.bfloat16)
+    name = lax.broadcasted_iota(jnp.int32, (DH, rows), 0)
+    at = lax.broadcasted_iota(jnp.int32, (DH, rows), 1)
+    named = (name.astype(jnp.float32) + 1.0 == seg_row) | ((name == OWN) & (at < text))
+    query_mask[...] = jnp.where(named, 1.0, 0.0).T.astype(jnp.bfloat16)
+    ahead = lax.broadcasted_iota(jnp.int32, (half, half), 0) > lax.broadcasted_iota(jnp.int32, (half, half), 1)
+    diagonal[...] = jnp.where(ahead, FAR, 0.0)
+    val_all[DH:, :] = jnp.ones_like(val_all[DH:, :])
     scale = LOG2E * DH ** -0.5
-    total = key_all.shape[0]
-
-    def attend(queries, heads, rows_from, rows_to, low, high):
-        count = rows_to - rows_from
-        scores = lax.dot_general(
-            queries, key_all[low:high], (((1,), (1,)), ((), ())), preferred_element_type=jnp.float32
+
+    def attend(queries, pieces):
+        scores = []
+        for low, high, extra in pieces:
+            piece = lax.dot_general(
+                key_all[low:high], queries, (((1,), (1,)), ((), ())), preferred_element_type=jnp.float32
+            )
+            scores.append(piece if extra is None else piece + extra)
+        largest = functools.reduce(jnp.maximum, [jnp.max(piece, axis=0, keepdims=True) for piece in scores])
+        weights = jnp.concatenate(
+            [jnp.exp2((piece - largest) * scale).astype(jnp.bfloat16) for piece in scores], axis=0
         )
-        scores = (scores.reshape(heads, count, high - low) + bias[rows_from:rows_to, low:high][None]).reshape(
-            heads * count, high - low
+        summed = jnp.dot(
+            val_all[:, pieces[0][0]:pieces[-1][1]], weights, preferred_element_type=jnp.float32
         )
-        largest = jnp.max(scores, axis=1, keepdims=True)
-        weights = jnp.exp2((scores - largest) * scale).astype(jnp.bfloat16)
-        summed = jnp.dot(weights, val_all[low:high], preferred_element_type=jnp.float32)
-        return summed[:, :DH] / summed[:, DH:]
-
+        return (summed[:DH] * (1.0 / summed[DH:DH + 1])).T
+
+    def turned(values):
+        return values.astype(jnp.float32).T.astype(jnp.bfloat16)
+
+    slot_end = slot_start + pad
     together = 2
+    tiles = (
+        (0, ((0, REACH * text, False), (REACH * text, slot_start, True), (slot_start, slot_end, False))),
+        (half, ((half, slot_end, False), (slot_end, total, True))),
+    )
     for group in range(groups):
         arrive(group, 1)
         arrive(group, 3)
         for place in range(REACH):
-            key_all[place * text:(place + 1) * text, :] = kv_buf[group, place, :, :DH]
-            val_all[place * text:(place + 1) * text, :DH] = kv_buf[group, place, :, DH:]
+            key_all[place * text:(place + 1) * text, :DH] = kv_buf[group, place, :, :DH]
+            val_all[:DH, place * text:(place + 1) * text] = turned(kv_buf[group, place, :, DH:])
         own = text_ref[group, :, query_width:]
-        key_all[REACH * text:slot_start, :] = own[:half, :DH]
-        val_all[REACH * text:slot_start, :DH] = own[:half, DH:]
-        key_all[slot_start + pad:, :] = own[half:, :DH]
-        val_all[slot_start + pad:, :DH] = own[half:, DH:]
-        for place in range(REACH + 1):
-            slot_rows = aux_buf[place, group * slot_count:(group + 1) * slot_count]
-            at = slot_start + place * slot_count
-            key_all[at:at + slot_count, :] = slot_rows[:, :DH]
-            val_all[at:at + slot_count, :DH] = slot_rows[:, DH:]
+        key_all[REACH * text:slot_start, :DH] = own[:half, :DH]
+        val_all[:DH, REACH * text:slot_start] = turned(own[:half, DH:])
+        key_all[slot_end:, :DH] = own[half:, :DH]
+        val_all[:DH, slot_end:] = turned(own[half:, DH:])
+        slot_rows = [aux_buf[place, group * slot_count:(group + 1) * slot_count] for place in range(REACH + 1)]
+        if spare:
+            slot_rows.append(jnp.zeros((spare, 2 * DH), jnp.bfloat16))
+        slot_rows = jnp.concatenate(slot_rows, axis=0)
+        key_all[slot_start:slot_end, :DH] = slot_rows[:, :DH]
+        val_all[:DH, slot_start:slot_end] = turned(slot_rows[:, DH:])
 
         def some_heads(index, carry):
             lanes = [pl.ds(pl.multiple_of((index * together + k) * DH, DH), DH) for k in range(together)]
-            for rows_from, low, high in ((0, 0, slot_start + pad), (half, half, total)):
+            wide = jnp.concatenate([diagonal[...]] * together, axis=1)
+            for first, pieces in tiles:
+                mask = query_mask[first:first + half]
                 queries = jnp.concatenate(
-                    [text_ref[group, rows_from:rows_from + half, lane] for lane in lanes], axis=0
+                    [
+                        jnp.concatenate([text_ref[group, first:first + half, lane], mask], axis=1)
+                        for lane in lanes
+                    ],
+                    axis=0,
                 )
-                result = attend(queries, together, rows_from, rows_from + half, low, high).astype(jnp.bfloat16)
+                result = attend(
+                    queries, [(low, high, wide if last else None) for low, high, last in pieces]
+                ).astype(jnp.bfloat16)
                 for k, lane in enumerate(lanes):
-                    out_ref[group, rows_from:rows_from + half, lane] = result[k * half:(k + 1) * half]
+                    out_ref[group, first:first + half, lane] = result[k * half:(k + 1) * half]
             return carry
 
         steps = GQ // together
@@ -287,12 +308,23 @@
                 relay_far(group + 2)
         lax.fori_loop(steps // 2, steps, some_heads, 0)
         slot_queries = slots[group * slot_count:(group + 1) * slot_count, :query_width].astype(jnp.bfloat16)
-        queries = jnp.concatenate([slot_queries[:, k * DH:(k + 1) * DH] for k in range(GQ)], axis=0)
-        result = attend(queries, GQ, text, rows, text, total)
-        live = live_col[...]
-        for k in range(GQ):
-            head = jnp.where(live > 0, result[k * slot_count:(k + 1) * slot_count], 0.0)
-            out_ref[group, text:, k * DH:(k + 1) * DH] = head.astype(jnp.bfloat16)
+        mask = query_mask[text:]
+        heads = max(1, min(GQ, 256 // slot_count))
+        for head in range(0, GQ, heads):
+            queries = jnp.concatenate(
+                [
+                    jnp.concatenate([slot_queries[:, k * DH:(k + 1) * DH], mask], axis=1)
+                    for k in range(head, head + heads)
+                ],
+                axis=0,
+            )
+            extra = slot_order_ref[:, head * slot_count:(head + heads) * slot_count]
+            result = attend(
+                queries, [(text, slot_start, None), (slot_start, slot_end, extra), (slot_end, total, None)]
+            )
+            for k in range(heads):
+                kept = jnp.where(live_col[...] > 0, result[k * slot_count:(k + 1) * slot_count], 0.0)
+                out_ref[group, text:, (head + k) * DH:(head + k + 1) * DH] = kept.astype(jnp.bfloat16)
 
     for item in range(groups + 1):
         finish(item, own_copies + far_copies + near_copies)
@@ -312,17 +344,6 @@
     vis_count = vis_rows.shape[0]
     vis_block = up(vis_count * groups, 16)
     text_t = text_rows.transpose(1, 0, 2)
-    listed = jnp.concatenate(
-        [
-            vis_rows,
-            jnp.broadcast_to(vis_dest[:, :, None].astype(jnp.bfloat16), (vis_count, vis_rows.shape[1], DH)),
-        ],
-        axis=2,
-    )
-    listed = listed.reshape(vis_count, n_shard, groups, width + DH).transpose(1, 0, 2, 3)
-    listed = listed.reshape(n_shard, vis_count * groups, width + DH)
-    listed = jnp.pad(listed, ((0, 0), (0, vis_block - vis_count * groups), (0, 0)))
-
     index = np.arange(n_shard * vis_block)
     within = index % vis_block
     valid = within < vis_count * groups
@@ -333,6 +354,8 @@
     slot = np.broadcast_to((place % slot_count)[:, None], pick.shape)
 
     pad = up((REACH + 1) * slot_count, 128)
+    own = np.arange(pad) - REACH * slot_count
+    behind = (own[:, None] > np.arange(GQ * slot_count)[None, :] % slot_count) & (own < slot_count)[:, None]
     keys = (REACH + 1) * text + pad
     aux_rows = groups * slot_count + 16
     n_source = n_seq * n_shard
@@ -340,15 +363,17 @@
     result = pl.pallas_call(
         functools.partial(kernel, n_group, n_seq, n_shard),
         out_shape=jax.ShapeDtypeStruct((groups, rows, GQ * DH), jnp.bfloat16),
-        in_specs=[vmem] * 7,
+        in_specs=[vmem] * 8,
         out_specs=vmem,
         scratch_shapes=[
             pltpu.VMEM((groups, REACH, text, 2 * DH), jnp.bfloat16),
             pltpu.VMEM((REACH + 1, aux_rows, 2 * DH), jnp.bfloat16),
+            pltpu.VMEM((n_shard, vis_block, width + DH), jnp.bfloat16),
             pltpu.VMEM((n_source, vis_block, width + DH), jnp.bfloat16),
-            pltpu.VMEM((keys, DH), jnp.bfloat16),
             pltpu.VMEM((keys, 2 * DH), jnp.bfloat16),
-            pltpu.VMEM((rows, keys), jnp.float32),
+            pltpu.VMEM((DH + 16, keys), jnp.bfloat16),
+            pltpu.VMEM((rows, DH), jnp.bfloat16),
+            pltpu.VMEM((text // 2, text // 2), jnp.float32),
             pltpu.VMEM((groups * slot_count, width), jnp.float32),
             pltpu.VMEM((slot_count, DH), jnp.float32),
             pltpu.SemaphoreType.DMA((groups + 1, 6)),
@@ -357,16 +382,17 @@
             pltpu.SemaphoreType.DMA((n_source,)),
         ],
         compiler_params=pltpu.CompilerParams(
-            collective_id=0, has_side_effects=True, vmem_limit_bytes=56 * 1024 * 1024
+            collective_id=0, has_side_effects=True, vmem_limit_bytes=36 * 1024 * 1024
         ),
     )(
         text_t,
-        listed,
-        segments[None, :],
-        segments[:, None],
+        vis_rows,
+        jnp.broadcast_to(vis_dest, (vis_count, DH)),
+        segments,
         jnp.asarray(same, jnp.float32),
         jnp.asarray(pick, jnp.float32),
         jnp.asarray(slot, jnp.float32),
+        jnp.asarray(np.where(behind, FAR, 0.0), jnp.float32),
     )
     return result.transpose(1, 0, 2)
 

time: 65.4 us -> 58.5 us (0.89)
  local copies, waits for them, and re-layouts: 11.7 us -> 5.95 us
  other arithmetic: 1.55 us -> 0 us
    broadcast_in_dim x3 -> x1, local copies, waits for them, and re-layouts: 2.74 us -> 0.72 us  [shards(): jnp.broadcast_to(vis_dest, (vis_count, DH))]
    transpose x1, local copies, waits for them, and re-layouts: 4.71 us -> 3.08 us  [shards(): return result.transpose(1, 0, 2)]
    unnamed x1 -> x13, local copies, waits for them, and re-layouts: 3.56 us -> 2.14 us
    concatenate x1 -> x0, other arithmetic: 0.9 us -> none  [shards(): jnp.concatenate([vis_rows, jnp.broadcast_to(vis_dest[:, :, None].astype(j...]
    reshape x3 -> x0, local copies, waits for them, and re-layouts: 0.72 us -> none  [the longest x1 0.66 us: shards(): listed = listed.reshape(n_shard, vis_count * groups, width + DH)]
    convert_element_type x1 -> x0, other arithmetic: 0.66 us -> none  [shards(): vis_dest[:, :, None].astype(jnp.bfloat16)]
where the time goes in v2:
time: 58.5 us; the launch traced here: 57.9 us
  Pallas kernels  51.9 us (89%)
  local copies, waits for them, and re-layouts  5.95 us (10%)
    pallas_call x1, Pallas kernels, shards(): pl.pallas_call(functools.partial(kernel, n_group, n_seq, n_shard), out_sh...  51.9 us
    transpose x1, local copies, waits for them, and re-layouts, shards(): return result.transpose(1, 0, 2)  3.08 us
    unnamed x13, local copies, waits for them, and re-layouts  2.14 us

profile of v2, /device:TPU:9, one launch (start us, length us, event | category | flops | bytes accessed | tf_op | source)
XLA Modules:
  0.0 57.9 jit_solution(17414965483532747342)
XLA Ops:
  0.0 0.7 %broadcast_in_dim.8.dest_ref = s32[4,128]{1,0:T(4,128)S(1)} broadcast(s32[4]{0:T(128)} %bitcast.7), dimensions={0} | broadcast | bytes 2064 | tf_op jit(solution)/shard_map/broadcast_in_dim | solution.py:390
  0.7 0.0 copy-start
  0.7 0.0 copy-start.1
  0.7 0.0 copy-start.2
  0.7 0.0 copy-start.3
  0.7 0.0 copy-start.4
  0.7 0.0 copy-start.5
  0.8 2.1 %copy.12 = bf16[256,4,1280]{2,0,1:T(8,128)(2,1)S(1)} copy(bf16[256,4,1280]{2,1,0:T(4,128)(2,1)} %param.8) | data formatting | bytes 5242880 | tf_op args[0]
  2.9 0.0 copy-done
  2.9 0.0 copy-done.1
  2.9 0.0 copy-done.2
  2.9 0.0 copy-done.3
  2.9 0.0 copy-done.4
  2.9 0.0 copy-done.5
  2.9 51.9 %shard_map.82 = bf16[4,272,1024]{2,1,0:T(8,128)(2,1)S(1)} custom-call(bf16[4,256,1280]{2,1,0:T(8,128)(2,1)S(1)} %bitcast.5, bf16[4,8,1280]{2,1,0:T(8,128)(2,1)S(1)} %copy-done, s32[4,128]{1,0:T(4,128)S(1)} %broadcast_in_dim.8.dest_ref, s32[272]{0:T(512)S(1)} %copy-done.5, f32[32,32]{1,0:T(8,128)S(1)} %copy-done.4, f32[64,32]{1,0:T(8,128)S(1)} %copy-done.3, ...), custom_call_target="tpu_custom_call" | custom-call | tf_op jit(solution)/shard_map/pallas_call | solution.py:363
  54.8 3.1 %copy.10 = bf16[272,4,1024]{2,1,0:T(4,128)(2,1)} copy(bf16[272,4,1024]{2,0,1:T(8,128)(2,1)S(1)} %bitcast.6) | data formatting | bytes 4456448 | tf_op jit(solution)/shard_map/transpose | solution.py:397
Async XLA Ops:
  0.7 2.2 %copy-start = (bf16[4,8,1280]{2,1,0:T(8,128)(2,1)S(1)}, bf16[4,8,1280]{2,1,0:T(8,128)(2,1)}, u32[]{:S(2)}) copy-start(bf16[4,8,1280]{2,1,0:T(8,128)(2,1)} %vis_ref.1) | copy-start | bytes 245764
  0.7 2.2 %copy-start.1 = (f32[128,128]{1,0:T(8,128)S(1)}, f32[128,128]{1,0:T(8,128)}, u32[]{:S(2)}) copy-start(f32[128,128]{1,0:T(8,128)} %constant.11.clone.slot_order_ref) | copy-start | bytes 196612
  0.7 2.2 %copy-start.2 = (f32[64,32]{1,0:T(8,128)S(1)}, f32[64,32]{1,0:T(8,128)}, u32[]{:S(2)}) copy-start(f32[64,32]{1,0:T(8,128)} %constant.10.clone.slot_ref) | copy-start | bytes 24580
  0.7 2.2 %copy-start.3 = (f32[64,32]{1,0:T(8,128)S(1)}, f32[64,32]{1,0:T(8,128)}, u32[]{:S(2)}) copy-start(f32[64,32]{1,0:T(8,128)} %constant.9.clone.pick_ref) | copy-start | bytes 24580
  0.7 2.2 %copy-start.4 = (f32[32,32]{1,0:T(8,128)S(1)}, f32[32,32]{1,0:T(8,128)}, u32[]{:S(2)}) copy-start(f32[32,32]{1,0:T(8,128)} %constant.8.clone.same_ref) | copy-start | bytes 12292
  0.7 2.2 %copy-start.5 = (s32[272]{0:T(512)S(1)}, s32[272]{0:T(512)}, u32[]{:S(2)}) copy-start(s32[272]{0:T(512)} %seg_ref.1) | copy-start | bytes 3268

commit v3 on v2

--- a/solution.py
+++ b/solution.py
@@ -26,6 +26,7 @@
 def kernel(
     n_group, n_seq, n_shard, text_ref, vis_ref, dest_ref, seg_ref, same_ref, pick_ref, slot_ref,
     slot_order_ref, out_ref, kv_buf, aux_buf, vis_stage, vis_buf, key_all, val_all, query_mask, diagonal, slots, live_col,
+    score_even, score_odd, weight_even, weight_odd,
     send_sem, recv_sem, vis_send, vis_recv,
 ):
     groups, text, width = text_ref.shape
@@ -87,13 +88,16 @@
 
     pl.semaphore_wait(barrier, n_source + 1 + (here + REACH < blocks).astype(jnp.int32))
 
+    def is_aux(item):
+        return isinstance(item, int) and item == groups
+
     def landing(item, place):
-        return aux_buf.at[place] if item == groups else kv_buf.at[item, place]
+        return aux_buf.at[place] if is_aux(item) else kv_buf.at[item, place]
 
     def source(item, place):
         if place < REACH:
             return landing(item, place)
-        if item == groups:
+        if is_aux(item):
             return aux_buf.at[REACH]
         return text_ref.at[item, :, pl.ds(query_width, 2 * DH)]
 
@@ -238,32 +242,62 @@
     val_all[DH:, :] = jnp.ones_like(val_all[DH:, :])
     scale = LOG2E * DH ** -0.5
 
-    def attend(queries, pieces):
-        scores = []
-        for low, high, extra in pieces:
-            piece = lax.dot_general(
-                key_all[low:high], queries, (((1,), (1,)), ((), ())), preferred_element_type=jnp.float32
-            )
-            scores.append(piece if extra is None else piece + extra)
-        largest = functools.reduce(jnp.maximum, [jnp.max(piece, axis=0, keepdims=True) for piece in scores])
-        weights = jnp.concatenate(
-            [jnp.exp2((piece - largest) * scale).astype(jnp.bfloat16) for piece in scores], axis=0
-        )
-        summed = jnp.dot(
-            val_all[:, pieces[0][0]:pieces[-1][1]], weights, preferred_element_type=jnp.float32
-        )
-        return (summed[:DH] * (1.0 / summed[DH:DH + 1])).T
-
     def turned(values):
         return values.astype(jnp.float32).T.astype(jnp.bfloat16)
 
     slot_end = slot_start + pad
     together = 2
-    tiles = (
-        (0, ((0, REACH * text, False), (REACH * text, slot_start, True), (slot_start, slot_end, False))),
-        (half, ((half, slot_end, False), (slot_end, total, True))),
-    )
-    for group in range(groups):
+    slot_heads = max(1, min(GQ, together * half // slot_count))
+    wide = jnp.concatenate([diagonal[...]] * together, axis=1)
+    first_pieces = ((0, REACH * text, None), (REACH * text, slot_start, wide), (slot_start, slot_end, None))
+    second_pieces = ((half, slot_end, None), (slot_end, total, wide))
+
+    def cut(pieces):
+        steps = []
+        for low, high, extra in pieces:
+            for at in range(low, high, 256):
+                end = min(at + 256, high)
+                steps.append((at, end, None if extra is None else extra[at - low:end - low]))
+        return steps
+
+    def text_tile(group, heads, first, pieces):
+        def queries():
+            mask = query_mask[first:first + half]
+            return jnp.concatenate(
+                [
+                    jnp.concatenate([text_ref[group, first:first + half, k * DH:(k + 1) * DH], mask], axis=1)
+                    for k in heads
+                ],
+                axis=0,
+            )
+
+        def store(result):
+            result = result.astype(jnp.bfloat16)
+            for number, k in enumerate(heads):
+                out_ref[group, first:first + half, k * DH:(k + 1) * DH] = result[number * half:(number + 1) * half]
+
+        return queries, cut(pieces), store
+
+    def slot_tile(group, heads):
+        extra = slot_order_ref[:, heads[0] * slot_count:(heads[-1] + 1) * slot_count]
+        pieces = ((text, slot_start, None), (slot_start, slot_end, extra), (slot_end, total, None))
+
+        def queries():
+            mask = query_mask[text:]
+            mine = pl.ds(pl.multiple_of(group * slot_count, slot_count), slot_count)
+            rows_of = [slots[mine, k * DH:(k + 1) * DH].astype(jnp.bfloat16) for k in heads]
+            return jnp.concatenate([jnp.concatenate([part, mask], axis=1) for part in rows_of], axis=0)
+
+        def store(result):
+            for number, k in enumerate(heads):
+                kept = jnp.where(live_col[...] > 0, result[number * slot_count:(number + 1) * slot_count], 0.0)
+                out_ref[group, text:, k * DH:(k + 1) * DH] = kept.astype(jnp.bfloat16)
+
+        return queries, cut(pieces), store
+
+    score_slots, weight_slots = (score_even, score_odd), (weight_even, weight_odd)
+
+    def one_group(group, carry):
         arrive(group, 1)
         arrive(group, 3)
         for place in range(REACH):
@@ -274,57 +308,96 @@
         val_all[:DH, REACH * text:slot_start] = turned(own[:half, DH:])
         key_all[slot_end:, :DH] = own[half:, :DH]
         val_all[:DH, slot_end:] = turned(own[half:, DH:])
-        slot_rows = [aux_buf[place, group * slot_count:(group + 1) * slot_count] for place in range(REACH + 1)]
+        mine = pl.ds(pl.multiple_of(group * slot_count, slot_count), slot_count)
+        slot_rows = [aux_buf[place, mine] for place in range(REACH + 1)]
         if spare:
             slot_rows.append(jnp.zeros((spare, 2 * DH), jnp.bfloat16))
         slot_rows = jnp.concatenate(slot_rows, axis=0)
         key_all[slot_start:slot_end, :DH] = slot_rows[:, :DH]
         val_all[:DH, slot_start:slot_end] = turned(slot_rows[:, DH:])
 
-        def some_heads(index, carry):
-            lanes = [pl.ds(pl.multiple_of((index * together + k) * DH, DH), DH) for k in range(together)]
-            wide = jnp.concatenate([diagonal[...]] * together, axis=1)
-            for first, pieces in tiles:
-                mask = query_mask[first:first + half]
-                queries = jnp.concatenate(
-                    [
-                        jnp.concatenate([text_ref[group, first:first + half, lane], mask], axis=1)
-                        for lane in lanes
-                    ],
-                    axis=0,
+        tiles = []
+        for head in range(0, GQ, together):
+            heads = range(head, head + together)
+            tiles.append(text_tile(group, heads, 0, first_pieces))
+            tiles.append(text_tile(group, heads, half, second_pieces))
+        for head in range(0, GQ, slot_heads):
+            tiles.append(slot_tile(group, range(head, head + slot_heads)))
+
+        def score_steps(number):
+            queries, steps, _ = tiles[number]
+            held = score_slots[number % 2]
+            state = {"queries": queries(), "largest": None}
+
+            def one(step):
+                low, high, extra = step
+                piece = lax.dot_general(
+                    key_all[low:high], state["queries"], (((1,), (1,)), ((), ())),
+                    preferred_element_type=jnp.float32,
                 )
-                result = attend(
-                    queries, [(low, high, wide if last else None) for low, high, last in pieces]
-                ).astype(jnp.bfloat16)
-                for k, lane in enumerate(lanes):
-                    out_ref[group, first:first + half, lane] = result[k * half:(k + 1) * half]
-            return carry
-
-        steps = GQ // together
-        lax.fori_loop(0, steps // 2, some_heads, 0)
-        if group + 1 < groups:
-            relay_near(group + 1)
-            if group + 2 < groups:
-                relay_far(group + 2)
-        lax.fori_loop(steps // 2, steps, some_heads, 0)
-        slot_queries = slots[group * slot_count:(group + 1) * slot_count, :query_width].astype(jnp.bfloat16)
-        mask = query_mask[text:]
-        heads = max(1, min(GQ, 256 // slot_count))
-        for head in range(0, GQ, heads):
-            queries = jnp.concatenate(
-                [
-                    jnp.concatenate([slot_queries[:, k * DH:(k + 1) * DH], mask], axis=1)
-                    for k in range(head, head + heads)
-                ],
-                axis=0,
+                if extra is not None:
+                    piece = piece + extra
+                at, lanes = low - steps[0][0], piece.shape[1]
+                held[at:at + high - low, :lanes] = piece
+                part = jnp.max(piece.reshape((high - low) // 8, 8, lanes), axis=0)
+                state["largest"] = part if state["largest"] is None else jnp.maximum(state["largest"], part)
+
+            return [functools.partial(one, step) for step in steps], state
+
+        def weight_steps(number, state):
+            steps = tiles[number][1]
+            held, made = score_slots[number % 2], weight_slots[number % 2]
+            lanes = state["largest"].shape[1]
+            largest = jnp.max(state["largest"], axis=0, keepdims=True)
+
+            def one(at, end):
+                made[at:end, :lanes] = jnp.exp2((held[at:end, :lanes] - largest) * scale).astype(jnp.bfloat16)
+
+            count = steps[-1][1] - steps[0][0]
+            return [functools.partial(one, at, min(at + 64, count)) for at in range(0, count, 64)], lanes
+
+        def finish_tile(number, lanes):
+            _, steps, store = tiles[number]
+            low, high = steps[0][0], steps[-1][1]
+            summed = jnp.dot(
+                val_all[:, low:high], weight_slots[number % 2][:high - low, :lanes],
+                preferred_element_type=jnp.float32,
             )
-            extra = slot_order_ref[:, head * slot_count:(head + heads) * slot_count]
-            result = attend(
-                queries, [(text, slot_start, None), (slot_start, slot_end, extra), (slot_end, total, None)]
-            )
-            for k in range(heads):
-                kept = jnp.where(live_col[...] > 0, result[k * slot_count:(k + 1) * slot_count], 0.0)
-                out_ref[group, text:, (head + k) * DH:(head + k + 1) * DH] = kept.astype(jnp.bfloat16)
+            store((summed[:DH] * (1.0 / summed[DH:DH + 1])).T)
+
+        work, state = score_steps(0)
+        for step in work:
+            step()
+        before = None
+        for number in range(len(tiles)):
+            if number == len(tiles) // 2:
+                @pl.when(group + 1 < groups)
+                def _():
+                    relay_near(group + 1)
+
+                @pl.when(group + 2 < groups)
+                def _():
+                    relay_far(group + 2)
+            if before is not None:
+                finish_tile(number - 1, before)
+            weigh, lanes = weight_steps(number, state)
+            score = []
+            if number + 1 < len(tiles):
+                score, state = score_steps(number + 1)
+            done = 0
+            for position, step in enumerate(score):
+                step()
+                until = (position + 1) * len(weigh) // len(score)
+                for part in weigh[done:until]:
+                    part()
+                done = until
+            for part in weigh[done:]:
+                part()
+            before = lanes
+        finish_tile(len(tiles) - 1, before)
+        return carry
+
+    lax.fori_loop(0, groups, one_group, 0)
 
     for item in range(groups + 1):
         finish(item, own_copies + far_copies + near_copies)
@@ -376,6 +449,10 @@
             pltpu.VMEM((text // 2, text // 2), jnp.float32),
             pltpu.VMEM((groups * slot_count, width), jnp.float32),
             pltpu.VMEM((slot_count, DH), jnp.float32),
+            pltpu.VMEM((keys - text // 2, text), jnp.float32),
+            pltpu.VMEM((keys - text // 2, text), jnp.float32),
+            pltpu.VMEM((keys - text // 2, text), jnp.bfloat16),
+            pltpu.VMEM((keys - text // 2, text), jnp.bfloat16),
             pltpu.SemaphoreType.DMA((groups + 1, 6)),
             pltpu.SemaphoreType.DMA((groups + 1, REACH)),
             pltpu.SemaphoreType.DMA((n_source,)),

time: 58.5 us -> 48.9 us (0.84)
  Pallas kernels: 51.9 us -> 42.4 us
    pallas_call x1, Pallas kernels: 51.9 us -> 42.4 us  [shards(): pl.pallas_call(functools.partial(kernel, n_group, n_seq, n_shard), out_sh...]
where the time goes in v3:
time: 48.9 us; the launch traced here: 48.4 us
  Pallas kernels  42.4 us (87%)
  local copies, waits for them, and re-layouts  5.95 us (12%)
    pallas_call x1, Pallas kernels, shards(): pl.pallas_call(functools.partial(kernel, n_group, n_seq, n_shard), out_sh...  42.4 us
    transpose x1, local copies, waits for them, and re-layouts, shards(): return result.transpose(1, 0, 2)  3.08 us
    unnamed x13, local copies, waits for them, and re-layouts  2.14 us

profile of v3, /device:TPU:9, one launch (start us, length us, event | category | flops | bytes accessed | tf_op | source)
XLA Modules:
  0.0 48.4 jit_solution(17340617755158032705)
XLA Ops:
  0.0 0.7 %broadcast_in_dim.8.dest_ref = s32[4,128]{1,0:T(4,128)S(1)} broadcast(s32[4]{0:T(128)} %bitcast.7), dimensions={0} | broadcast | bytes 2064 | tf_op jit(solution)/shard_map/broadcast_in_dim | solution.py:467
  0.7 0.0 copy-start
  0.7 0.0 copy-start.1
  0.7 0.0 copy-start.2
  0.7 0.0 copy-start.3
  0.7 0.0 copy-start.4
  0.7 0.0 copy-start.5
  0.8 2.1 %copy.12 = bf16[256,4,1280]{2,0,1:T(8,128)(2,1)S(1)} copy(bf16[256,4,1280]{2,1,0:T(4,128)(2,1)} %param.8) | data formatting | bytes 5242880 | tf_op args[0]
  2.9 0.0 copy-done
  2.9 0.0 copy-done.1
  2.9 0.0 copy-done.2
  2.9 0.0 copy-done.3
  2.9 0.0 copy-done.4
  2.9 0.0 copy-done.5
  2.9 42.4 %shard_map.82 = bf16[4,272,1024]{2,1,0:T(8,128)(2,1)S(1)} custom-call(bf16[4,256,1280]{2,1,0:T(8,128)(2,1)S(1)} %bitcast.5, bf16[4,8,1280]{2,1,0:T(8,128)(2,1)S(1)} %copy-done, s32[4,128]{1,0:T(4,128)S(1)} %broadcast_in_dim.8.dest_ref, s32[272]{0:T(512)S(1)} %copy-done.5, f32[32,32]{1,0:T(8,128)S(1)} %copy-done.4, f32[64,32]{1,0:T(8,128)S(1)} %copy-done.3, ...), custom_call_target="tpu_custom_call" | custom-call | tf_op jit(solution)/shard_map/pallas_call | solution.py:436
  45.3 3.1 %copy.10 = bf16[272,4,1024]{2,1,0:T(4,128)(2,1)} copy(bf16[272,4,1024]{2,0,1:T(8,128)(2,1)S(1)} %bitcast.6) | data formatting | bytes 4456448 | tf_op jit(solution)/shard_map/transpose | solution.py:474
Async XLA Ops:
  0.7 2.2 %copy-start = (bf16[4,8,1280]{2,1,0:T(8,128)(2,1)S(1)}, bf16[4,8,1280]{2,1,0:T(8,128)(2,1)}, u32[]{:S(2)}) copy-start(bf16[4,8,1280]{2,1,0:T(8,128)(2,1)} %vis_ref.1) | copy-start | bytes 245764
  0.7 2.2 %copy-start.1 = (f32[128,128]{1,0:T(8,128)S(1)}, f32[128,128]{1,0:T(8,128)}, u32[]{:S(2)}) copy-start(f32[128,128]{1,0:T(8,128)} %constant.11.clone.slot_order_ref) | copy-start | bytes 196612
  0.7 2.2 %copy-start.2 = (f32[64,32]{1,0:T(8,128)S(1)}, f32[64,32]{1,0:T(8,128)}, u32[]{:S(2)}) copy-start(f32[64,32]{1,0:T(8,128)} %constant.10.clone.slot_ref) | copy-start | bytes 24580
  0.7 2.2 %copy-start.3 = (f32[64,32]{1,0:T(8,128)S(1)}, f32[64,32]{1,0:T(8,128)}, u32[]{:S(2)}) copy-start(f32[64,32]{1,0:T(8,128)} %constant.9.clone.pick_ref) | copy-start | bytes 24580
  0.7 2.2 %copy-start.4 = (f32[32,32]{1,0:T(8,128)S(1)}, f32[32,32]{1,0:T(8,128)}, u32[]{:S(2)}) copy-start(f32[32,32]{1,0:T(8,128)} %constant.8.clone.same_ref) | copy-start | bytes 12292
  0.7 2.2 %copy-start.5 = (s32[272]{0:T(512)S(1)}, s32[272]{0:T(512)}, u32[]{:S(2)}) copy-start(s32[272]{0:T(512)} %seg_ref.1) | copy-start | bytes 3268

commit v4 on v3

--- a/solution.py
+++ b/solution.py
@@ -25,9 +25,10 @@
 
 def kernel(
     n_group, n_seq, n_shard, text_ref, vis_ref, dest_ref, seg_ref, same_ref, pick_ref, slot_ref,
-    slot_order_ref, out_ref, kv_buf, aux_buf, vis_stage, vis_buf, key_all, val_all, query_mask, diagonal, slots, live_col,
+    slot_order_ref, out_ref, kv_buf, aux_buf, key_stage, key_listed, query_stage, query_listed, placed, key_all, val_all,
+    text_mask, slot_mask, diagonal, slots, live_col,
     score_even, score_odd, weight_even, weight_odd,
-    send_sem, recv_sem, vis_send, vis_recv,
+    send_sem, recv_sem, key_send, key_recv, query_send, query_recv,
 ):
     groups, text, width = text_ref.shape
     query_width = GQ * DH
@@ -36,7 +37,7 @@
     half = text // 2
     pad = key_all.shape[0] - (REACH + 1) * text
     slot_start = REACH * text + half
-    vis_count, vis_block = vis_ref.shape[0], vis_stage.shape[1]
+    vis_count, vis_block = vis_ref.shape[0], key_stage.shape[1]
     n_source = n_seq * n_shard
     blocks = n_group * n_seq
     aux_rows = groups * slot_count
@@ -65,8 +66,10 @@
         if vis_block > vis_count * groups:
             listed.append(jnp.zeros((vis_block - vis_count * groups, width), jnp.float32))
             names.append(jnp.zeros((vis_block - vis_count * groups, DH), jnp.float32))
-        vis_stage[shard, :, :width] = jnp.concatenate(listed, axis=0).astype(jnp.bfloat16)
-        vis_stage[shard, :, width:] = jnp.concatenate(names, axis=0).astype(jnp.bfloat16)
+        listed = jnp.concatenate(listed, axis=0).astype(jnp.bfloat16)
+        query_stage[shard] = listed[:, :query_width]
+        key_stage[shard, :, :2 * DH] = listed[:, query_width:]
+        key_stage[shard, :, 2 * DH:] = jnp.concatenate(names, axis=0).astype(jnp.bfloat16)
 
     def greet(step, carry):
         pl.semaphore_signal(barrier, inc=1, device_id=peer(lax.rem(me + step, n_source)), device_id_type=MESH)
@@ -150,48 +153,64 @@
         arrive(item, 2)
         start(item, near_copies)
 
-    def vis_copy(step, landing_index):
+    def vis_copy(parts, step, landing_index):
+        stage, listed, sent, received = parts
         target = lax.rem(me + step, n_source)
         return pltpu.make_async_remote_copy(
-            src_ref=vis_stage.at[lax.rem(target, n_shard)],
-            dst_ref=vis_buf.at[landing_index],
-            send_sem=vis_send.at[step],
-            recv_sem=vis_recv.at[step],
+            src_ref=stage.at[lax.rem(target, n_shard)],
+            dst_ref=listed.at[landing_index],
+            send_sem=sent.at[step],
+            recv_sem=received.at[step],
             device_id=peer(target),
             device_id_type=MESH,
         )
 
-    def vis_start(step, carry):
-        vis_copy(step, me).start()
-        return carry
-
-    lax.fori_loop(1, n_source, vis_start, 0)
-    for item in range(groups):
-        start(item, own_copies)
-    vis_buf[me] = vis_stage[my_shard]
-
-    def vis_wait(step, carry):
-        vis_copy(step, lax.rem(me + n_source - step, n_source)).wait_recv()
-        return carry
-
-    lax.fori_loop(1, n_source, vis_wait, 0)
+    def vis_start(parts):
+        def one(step, carry):
+            vis_copy(parts, step, me).start()
+            return carry
+
+        lax.fori_loop(1, n_source, one, 0)
+        parts[1][me] = parts[0][my_shard]
+
+    def vis_wait(parts):
+        def one(step, carry):
+            vis_copy(parts, step, lax.rem(me + n_source - step, n_source)).wait_recv()
+            return carry
+
+        lax.fori_loop(1, n_source, one, 0)
+
+    def vis_finish(parts):
+        def one(step, carry):
+            vis_copy(parts, step, me).wait_send()
+            return carry
+
+        lax.fori_loop(1, n_source, one, 0)
+
+    key_parts = (key_stage, key_listed, key_send, key_recv)
+    query_parts = (query_stage, query_listed, query_send, query_recv)
+    vis_start(key_parts)
+    start(0, own_copies)
+    vis_wait(key_parts)
 
     block_rows = n_shard * vis_block
     my_dest = my_seq.astype(jnp.float32)
     filled = jnp.zeros((aux_rows, 1), jnp.float32)
     for seq in range(n_seq):
-        listed = vis_buf[seq * n_shard:(seq + 1) * n_shard].reshape(block_rows, width + DH)
-        dest = listed[:, width:].astype(jnp.float32)
+        listed = key_listed[seq * n_shard:(seq + 1) * n_shard].reshape(block_rows, 3 * DH)
+        dest = listed[:, 2 * DH:].astype(jnp.float32)
         dest_across = dest.T[0:1, :]
         earlier = jnp.where(dest[:, 0:1] == dest_across, same_ref[...], 0.0)
         rank = jnp.sum(earlier, axis=0, keepdims=True)
         placing = jnp.where(
             (slot_ref[...] == rank + float(seq * CAP)) & (dest_across == my_dest), pick_ref[...], 0.0
         )
-        part = jnp.dot(placing.astype(jnp.bfloat16), listed[:, :width], preferred_element_type=jnp.float32)
-        slots[...] = part if seq == 0 else slots[...] + part
-        filled = filled + jnp.sum(placing, axis=1, keepdims=True)
-    aux_buf[REACH, 0:aux_rows] = slots[:, query_width:].astype(jnp.bfloat16)
+        placing = placing.astype(jnp.bfloat16)
+        placed[:, seq * block_rows:(seq + 1) * block_rows] = placing
+        part = jnp.dot(placing, listed[:, :2 * DH], preferred_element_type=jnp.float32)
+        slot_keys = part if seq == 0 else slot_keys + part
+        filled = filled + jnp.sum(placing.astype(jnp.float32), axis=1, keepdims=True)
+    aux_buf[REACH, 0:aux_rows] = slot_keys.astype(jnp.bfloat16)
     live_col[...] = jnp.broadcast_to(filled[:slot_count], live_col.shape)
     live_across = live_col[...].T[0:1, :]
     seg_row = seg_ref[...].reshape(1, rows).astype(jnp.float32) + 1.0
@@ -208,6 +227,9 @@
     )
     aux_buf[REACH, aux_rows:] = tag_rows.astype(jnp.bfloat16)
     start(groups, own_copies)
+    vis_start(query_parts)
+    for item in range(1, groups):
+        start(item, own_copies)
 
     relay_far(0)
     relay_far(groups)
@@ -233,10 +255,15 @@
     differs = (name < OWN) & (name.astype(jnp.float32) + 1.0 != tags)
     own_slot = (name == OWN) & (at >= 0) & (at < slot_count)
     key_all[:, DH:] = jnp.where(differs | own_slot, FAR, 0.0).T.astype(jnp.bfloat16)
+    together = 2
+    slot_heads = max(1, min(GQ, together * half // slot_count))
     name = lax.broadcasted_iota(jnp.int32, (DH, rows), 0)
     at = lax.broadcasted_iota(jnp.int32, (DH, rows), 1)
-    named = (name.astype(jnp.float32) + 1.0 == seg_row) | ((name == OWN) & (at < text))
-    query_mask[...] = jnp.where(named, 1.0, 0.0).T.astype(jnp.bfloat16)
+    named = jnp.where((name.astype(jnp.float32) + 1.0 == seg_row) | ((name == OWN) & (at < text)), 1.0, 0.0)
+    for part in range(2):
+        narrow = named[:, part * half:(part + 1) * half].astype(jnp.bfloat16)
+        text_mask[part] = jnp.concatenate([narrow] * together, axis=1)
+    slot_mask[...] = jnp.concatenate([named[:, text:]] * slot_heads, axis=1).astype(jnp.bfloat16)
     ahead = lax.broadcasted_iota(jnp.int32, (half, half), 0) > lax.broadcasted_iota(jnp.int32, (half, half), 1)
     diagonal[...] = jnp.where(ahead, FAR, 0.0)
     val_all[DH:, :] = jnp.ones_like(val_all[DH:, :])
@@ -246,55 +273,43 @@
         return values.astype(jnp.float32).T.astype(jnp.bfloat16)
 
     slot_end = slot_start + pad
-    together = 2
-    slot_heads = max(1, min(GQ, together * half // slot_count))
     wide = jnp.concatenate([diagonal[...]] * together, axis=1)
-    first_pieces = ((0, REACH * text, None), (REACH * text, slot_start, wide), (slot_start, slot_end, None))
-    second_pieces = ((half, slot_end, None), (slot_end, total, wide))
-
-    def cut(pieces):
-        steps = []
-        for low, high, extra in pieces:
-            for at in range(low, high, 256):
-                end = min(at + 256, high)
-                steps.append((at, end, None if extra is None else extra[at - low:end - low]))
-        return steps
-
-    def text_tile(group, heads, first, pieces):
+    first_span = (0, slot_end, REACH * text, slot_start, wide)
+    second_span = (half, total, slot_end, total, wide)
+
+    def text_tile(group, heads, part, span):
+        mine = slice(part * half, (part + 1) * half)
+
         def queries():
-            mask = query_mask[first:first + half]
-            return jnp.concatenate(
-                [
-                    jnp.concatenate([text_ref[group, first:first + half, k * DH:(k + 1) * DH], mask], axis=1)
-                    for k in heads
-                ],
-                axis=0,
-            )
+            rows_of = [text_ref[group, mine, k * DH:(k + 1) * DH] for k in heads]
+            return jnp.concatenate([turned(jnp.concatenate(rows_of, axis=0)), text_mask[part]], axis=0)
 
         def store(result):
             result = result.astype(jnp.bfloat16)
             for number, k in enumerate(heads):
-                out_ref[group, first:first + half, k * DH:(k + 1) * DH] = result[number * half:(number + 1) * half]
-
-        return queries, cut(pieces), store
+                out_ref[group, mine, k * DH:(k + 1) * DH] = result[number * half:(number + 1) * half]
+
+        return queries, span, store
 
     def slot_tile(group, heads):
         extra = slot_order_ref[:, heads[0] * slot_count:(heads[-1] + 1) * slot_count]
-        pieces = ((text, slot_start, None), (slot_start, slot_end, extra), (slot_end, total, None))
 
         def queries():
-            mask = query_mask[text:]
             mine = pl.ds(pl.multiple_of(group * slot_count, slot_count), slot_count)
-            rows_of = [slots[mine, k * DH:(k + 1) * DH].astype(jnp.bfloat16) for k in heads]
-            return jnp.concatenate([jnp.concatenate([part, mask], axis=1) for part in rows_of], axis=0)
+            rows_of = [slots[mine, k * DH:(k + 1) * DH] for k in heads]
+            return jnp.concatenate([turned(jnp.concatenate(rows_of, axis=0)), slot_mask[...]], axis=0)
 
         def store(result):
             for number, k in enumerate(heads):
                 kept = jnp.where(live_col[...] > 0, result[number * slot_count:(number + 1) * slot_count], 0.0)
                 out_ref[group, text:, k * DH:(k + 1) * DH] = kept.astype(jnp.bfloat16)
 
-        return queries, cut(pieces), store
-
+        return queries, (text, total, slot_start, slot_end, extra), store
+
+    vis_wait(query_parts)
+    slots[...] = jnp.dot(
+        placed[...], query_listed[...].reshape(n_source * vis_block, query_width), preferred_element_type=jnp.float32
+    )
     score_slots, weight_slots = (score_even, score_odd), (weight_even, weight_odd)
 
     def one_group(group, carry):
@@ -319,33 +334,32 @@
         tiles = []
         for head in range(0, GQ, together):
             heads = range(head, head + together)
-            tiles.append(text_tile(group, heads, 0, first_pieces))
-            tiles.append(text_tile(group, heads, half, second_pieces))
+            tiles.append(text_tile(group, heads, 0, first_span))
+            tiles.append(text_tile(group, heads, 1, second_span))
         for head in range(0, GQ, slot_heads):
             tiles.append(slot_tile(group, range(head, head + slot_heads)))
 
         def score_steps(number):
-            queries, steps, _ = tiles[number]
+            queries, (low, high, extra_low, extra_high, extra), _ = tiles[number]
             held = score_slots[number % 2]
             state = {"queries": queries(), "largest": None}
 
-            def one(step):
-                low, high, extra = step
-                piece = lax.dot_general(
-                    key_all[low:high], state["queries"], (((1,), (1,)), ((), ())),
-                    preferred_element_type=jnp.float32,
-                )
-                if extra is not None:
-                    piece = piece + extra
-                at, lanes = low - steps[0][0], piece.shape[1]
-                held[at:at + high - low, :lanes] = piece
-                part = jnp.max(piece.reshape((high - low) // 8, 8, lanes), axis=0)
-                state["largest"] = part if state["largest"] is None else jnp.maximum(state["largest"], part)
-
-            return [functools.partial(one, step) for step in steps], state
+            def one(start_at, end_at):
+                result = jnp.dot(key_all[start_at:end_at], state["queries"], preferred_element_type=jnp.float32)
+                lanes = result.shape[1]
+                for at in range(start_at, end_at, 128):
+                    piece = result[at - start_at:at - start_at + 128]
+                    if extra_low <= at < extra_high:
+                        piece = piece + extra[at - extra_low:at - extra_low + 128]
+                    held[at - low:at - low + 128, :lanes] = piece
+                    part = jnp.max(piece.reshape(16, 8, lanes), axis=0)
+                    state["largest"] = part if state["largest"] is None else jnp.maximum(state["largest"], part)
+
+            middle = low + (high - low) // 256 * 128
+            return [functools.partial(one, low, middle), functools.partial(one, middle, high)], state
 
         def weight_steps(number, state):
-            steps = tiles[number][1]
+            low, high = tiles[number][1][:2]
             held, made = score_slots[number % 2], weight_slots[number % 2]
             lanes = state["largest"].shape[1]
             largest = jnp.max(state["largest"], axis=0, keepdims=True)
@@ -353,12 +367,11 @@
             def one(at, end):
                 made[at:end, :lanes] = jnp.exp2((held[at:end, :lanes] - largest) * scale).astype(jnp.bfloat16)
 
-            count = steps[-1][1] - steps[0][0]
+            count = high - low
             return [functools.partial(one, at, min(at + 64, count)) for at in range(0, count, 64)], lanes
 
         def finish_tile(number, lanes):
-            _, steps, store = tiles[number]
-            low, high = steps[0][0], steps[-1][1]
+            _, (low, high, *_), store = tiles[number]
             summed = jnp.dot(
                 val_all[:, low:high], weight_slots[number % 2][:high - low, :lanes],
                 preferred_element_type=jnp.float32,
@@ -402,11 +415,8 @@
     for item in range(groups + 1):
         finish(item, own_copies + far_copies + near_copies)
 
-    def vis_finish(step, carry):
-        vis_copy(step, me).wait_send()
-        return carry
-
-    lax.fori_loop(1, n_source, vis_finish, 0)
+    vis_finish(key_parts)
+    vis_finish(query_parts)
 
 
 def shards(mesh_shape, text_rows, vis_rows, vis_dest, segments):
@@ -441,13 +451,17 @@
         scratch_shapes=[
             pltpu.VMEM((groups, REACH, text, 2 * DH), jnp.bfloat16),
             pltpu.VMEM((REACH + 1, aux_rows, 2 * DH), jnp.bfloat16),
-            pltpu.VMEM((n_shard, vis_block, width + DH), jnp.bfloat16),
-            pltpu.VMEM((n_source, vis_block, width + DH), jnp.bfloat16),
+            pltpu.VMEM((n_shard, vis_block, 3 * DH), jnp.bfloat16),
+            pltpu.VMEM((n_source, vis_block, 3 * DH), jnp.bfloat16),
+            pltpu.VMEM((n_shard, vis_block, GQ * DH), jnp.bfloat16),
+            pltpu.VMEM((n_source, vis_block, GQ * DH), jnp.bfloat16),
+            pltpu.VMEM((groups * slot_count, n_source * vis_block), jnp.bfloat16),
             pltpu.VMEM((keys, 2 * DH), jnp.bfloat16),
             pltpu.VMEM((DH + 16, keys), jnp.bfloat16),
-            pltpu.VMEM((rows, DH), jnp.bfloat16),
+            pltpu.VMEM((2, DH, text), jnp.bfloat16),
+            pltpu.VMEM((DH, min(GQ * slot_count, text)), jnp.bfloat16),
             pltpu.VMEM((text // 2, text // 2), jnp.float32),
-            pltpu.VMEM((groups * slot_count, width), jnp.float32),
+            pltpu.VMEM((groups * slot_count, GQ * DH), jnp.float32),
             pltpu.VMEM((slot_count, DH), jnp.float32),
             pltpu.VMEM((keys - text // 2, text), jnp.float32),
             pltpu.VMEM((keys - text // 2, text), jnp.float32),
@@ -455,6 +469,8 @@
             pltpu.VMEM((keys - text // 2, text), jnp.bfloat16),
             pltpu.SemaphoreType.DMA((groups + 1, 6)),
             pltpu.SemaphoreType.DMA((groups + 1, REACH)),
+            pltpu.SemaphoreType.DMA((n_source,)),
+            pltpu.SemaphoreType.DMA((n_source,)),
             pltpu.SemaphoreType.DMA((n_source,)),
             pltpu.SemaphoreType.DMA((n_source,)),
         ],

time: 48.9 us -> 42.6 us (0.87)
  Pallas kernels: 42.4 us -> 36.4 us
    pallas_call x1, Pallas kernels: 42.4 us -> 36.4 us  [shards(): pl.pallas_call(functools.partial(kernel, n_group, n_seq, n_shard), out_sh...]
where the time goes in v4:
time: 42.6 us; the launch traced here: 42.4 us
  Pallas kernels  36.4 us (85%)
  local copies, waits for them, and re-layouts  5.95 us (14%)
    pallas_call x1, Pallas kernels, shards(): pl.pallas_call(functools.partial(kernel, n_group, n_seq, n_shard), out_sh...  36.4 us
    transpose x1, local copies, waits for them, and re-layouts, shards(): return result.transpose(1, 0, 2)  3.08 us
    unnamed x13, local copies, waits for them, and re-layouts  2.14 us

profile of v4, /device:TPU:9, one launch (start us, length us, event | category | flops | bytes accessed | tf_op | source)
XLA Modules:
  0.0 42.4 jit_solution(13236961834990681303)
XLA Ops:
  0.0 0.7 %broadcast_in_dim.8.dest_ref = s32[4,128]{1,0:T(4,128)S(1)} broadcast(s32[4]{0:T(128)} %bitcast.7), dimensions={0} | broadcast | bytes 2064 | tf_op jit(solution)/shard_map/broadcast_in_dim | solution.py:483
  0.7 0.0 copy-start
  0.7 0.0 copy-start.1
  0.7 0.0 copy-start.2
  0.7 0.0 copy-start.3
  0.7 0.0 copy-start.4
  0.7 0.0 copy-start.5
  0.8 2.1 %copy.12 = bf16[256,4,1280]{2,0,1:T(8,128)(2,1)S(1)} copy(bf16[256,4,1280]{2,1,0:T(4,128)(2,1)} %param.8) | data formatting | bytes 5242880 | tf_op args[0]
  2.9 0.0 copy-done
  2.9 0.0 copy-done.1
  2.9 0.0 copy-done.2
  2.9 0.0 copy-done.3
  2.9 0.0 copy-done.4
  2.9 0.0 copy-done.5
  2.9 36.4 %shard_map.82 = bf16[4,272,1024]{2,1,0:T(8,128)(2,1)S(1)} custom-call(bf16[4,256,1280]{2,1,0:T(8,128)(2,1)S(1)} %bitcast.5, bf16[4,8,1280]{2,1,0:T(8,128)(2,1)S(1)} %copy-done, s32[4,128]{1,0:T(4,128)S(1)} %broadcast_in_dim.8.dest_ref, s32[272]{0:T(512)S(1)} %copy-done.5, f32[32,32]{1,0:T(8,128)S(1)} %copy-done.4, f32[64,32]{1,0:T(8,128)S(1)} %copy-done.3, ...), custom_call_target="tpu_custom_call" | custom-call | tf_op jit(solution)/shard_map/pallas_call | solution.py:446
  39.4 3.1 %copy.10 = bf16[272,4,1024]{2,1,0:T(4,128)(2,1)} copy(bf16[272,4,1024]{2,0,1:T(8,128)(2,1)S(1)} %bitcast.6) | data formatting | bytes 4456448 | tf_op jit(solution)/shard_map/transpose | solution.py:490
Async XLA Ops:
  0.7 2.2 %copy-start = (bf16[4,8,1280]{2,1,0:T(8,128)(2,1)S(1)}, bf16[4,8,1280]{2,1,0:T(8,128)(2,1)}, u32[]{:S(2)}) copy-start(bf16[4,8,1280]{2,1,0:T(8,128)(2,1)} %vis_ref.1) | copy-start | bytes 245764
  0.7 2.2 %copy-start.1 = (f32[128,128]{1,0:T(8,128)S(1)}, f32[128,128]{1,0:T(8,128)}, u32[]{:S(2)}) copy-start(f32[128,128]{1,0:T(8,128)} %constant.11.clone.slot_order_ref) | copy-start | bytes 196612
  0.7 2.2 %copy-start.2 = (f32[64,32]{1,0:T(8,128)S(1)}, f32[64,32]{1,0:T(8,128)}, u32[]{:S(2)}) copy-start(f32[64,32]{1,0:T(8,128)} %constant.10.clone.slot_ref) | copy-start | bytes 24580
  0.7 2.2 %copy-start.3 = (f32[64,32]{1,0:T(8,128)S(1)}, f32[64,32]{1,0:T(8,128)}, u32[]{:S(2)}) copy-start(f32[64,32]{1,0:T(8,128)} %constant.9.clone.pick_ref) | copy-start | bytes 24580
  0.7 2.2 %copy-start.4 = (f32[32,32]{1,0:T(8,128)S(1)}, f32[32,32]{1,0:T(8,128)}, u32[]{:S(2)}) copy-start(f32[32,32]{1,0:T(8,128)} %constant.8.clone.same_ref) | copy-start | bytes 12292
  0.7 2.2 %copy-start.5 = (s32[272]{0:T(512)S(1)}, s32[272]{0:T(512)}, u32[]{:S(2)}) copy-start(s32[272]{0:T(512)} %seg_ref.1) | copy-start | bytes 3268

commit v5 on v4

--- a/solution.py
+++ b/solution.py
@@ -15,6 +15,7 @@
 REACH = 4
 FAR = -(2.0 ** 100)
 OWN = 120
+TOGETHER = 4
 LOG2E = math.log2(math.e)
 MESH = pl.DeviceIdType.MESH
 
@@ -255,7 +256,7 @@
     differs = (name < OWN) & (name.astype(jnp.float32) + 1.0 != tags)
     own_slot = (name == OWN) & (at >= 0) & (at < slot_count)
     key_all[:, DH:] = jnp.where(differs | own_slot, FAR, 0.0).T.astype(jnp.bfloat16)
-    together = 2
+    together = text_mask.shape[2] // half
     slot_heads = max(1, min(GQ, together * half // slot_count))
     name = lax.broadcasted_iota(jnp.int32, (DH, rows), 0)
     at = lax.broadcasted_iota(jnp.int32, (DH, rows), 1)
@@ -332,12 +333,12 @@
         val_all[:DH, slot_start:slot_end] = turned(slot_rows[:, DH:])
 
         tiles = []
+        for head in range(0, GQ, slot_heads):
+            tiles.append(slot_tile(group, range(head, head + slot_heads)))
         for head in range(0, GQ, together):
             heads = range(head, head + together)
             tiles.append(text_tile(group, heads, 0, first_span))
             tiles.append(text_tile(group, heads, 1, second_span))
-        for head in range(0, GQ, slot_heads):
-            tiles.append(slot_tile(group, range(head, head + slot_heads)))
 
         def score_steps(number):
             queries, (low, high, extra_low, extra_high, extra), _ = tiles[number]
@@ -442,6 +443,7 @@
     keys = (REACH + 1) * text + pad
     aux_rows = groups * slot_count + 16
     n_source = n_seq * n_shard
+    lanes = TOGETHER * (text // 2)
     vmem = pl.BlockSpec(memory_space=pltpu.VMEM)
     result = pl.pallas_call(
         functools.partial(kernel, n_group, n_seq, n_shard),
@@ -458,15 +460,15 @@
             pltpu.VMEM((groups * slot_count, n_source * vis_block), jnp.bfloat16),
             pltpu.VMEM((keys, 2 * DH), jnp.bfloat16),
             pltpu.VMEM((DH + 16, keys), jnp.bfloat16),
-            pltpu.VMEM((2, DH, text), jnp.bfloat16),
-            pltpu.VMEM((DH, min(GQ * slot_count, text)), jnp.bfloat16),
+            pltpu.VMEM((2, DH, lanes), jnp.bfloat16),
+            pltpu.VMEM((DH, min(GQ * slot_count, lanes)), jnp.bfloat16),
             pltpu.VMEM((text // 2, text // 2), jnp.float32),
             pltpu.VMEM((groups * slot_count, GQ * DH), jnp.float32),
             pltpu.VMEM((slot_count, DH), jnp.float32),
-            pltpu.VMEM((keys - text // 2, text), jnp.float32),
-            pltpu.VMEM((keys - text // 2, text), jnp.float32),
-            pltpu.VMEM((keys - text // 2, text), jnp.bfloat16),
-            pltpu.VMEM((keys - text // 2, text), jnp.bfloat16),
+            pltpu.VMEM((keys - text // 2, lanes), jnp.float32),
+            pltpu.VMEM((keys - text // 2, lanes), jnp.float32),
+            pltpu.VMEM((keys - text // 2, lanes), jnp.bfloat16),
+            pltpu.VMEM((keys - text // 2, lanes), jnp.bfloat16),
             pltpu.SemaphoreType.DMA((groups + 1, 6)),
             pltpu.SemaphoreType.DMA((groups + 1, REACH)),
             pltpu.SemaphoreType.DMA((n_source,)),

time: 42.6 us -> 42.7 us (level)
  no operation moved by 1% of the time
where the time goes in v5:
time: 42.7 us; the launch traced here: 42.5 us
  Pallas kernels  36.5 us (85%)
  local copies, waits for them, and re-layouts  5.95 us (14%)
    pallas_call x1, Pallas kernels, shards(): pl.pallas_call(functools.partial(kernel, n_group, n_seq, n_shard), out_sh...  36.5 us
    transpose x1, local copies, waits for them, and re-layouts, shards(): return result.transpose(1, 0, 2)  3.08 us
    unnamed x13, local copies, waits for them, and re-layouts  2.14 us

profile of v5, /device:TPU:9, one launch (start us, length us, event | category | flops | bytes accessed | tf_op | source)
XLA Modules:
  0.0 42.5 jit_solution(562218177620990503)
XLA Ops:
  0.0 0.7 %broadcast_in_dim.8.dest_ref = s32[4,128]{1,0:T(4,128)S(1)} broadcast(s32[4]{0:T(128)} %bitcast.7), dimensions={0} | broadcast | bytes 2064 | tf_op jit(solution)/shard_map/broadcast_in_dim | solution.py:485
  0.7 0.0 copy-start
  0.7 0.0 copy-start.1
  0.7 0.0 copy-start.2
  0.7 0.0 copy-start.3
  0.7 0.0 copy-start.4
  0.7 0.0 copy-start.5
  0.8 2.1 %copy.12 = bf16[256,4,1280]{2,0,1:T(8,128)(2,1)S(1)} copy(bf16[256,4,1280]{2,1,0:T(4,128)(2,1)} %param.8) | data formatting | bytes 5242880 | tf_op args[0]
  2.9 0.0 copy-done
  2.9 0.0 copy-done.1
  2.9 0.0 copy-done.2
  2.9 0.0 copy-done.3
  2.9 0.0 copy-done.4
  2.9 0.0 copy-done.5
  2.9 36.5 %shard_map.82 = bf16[4,272,1024]{2,1,0:T(8,128)(2,1)S(1)} custom-call(bf16[4,256,1280]{2,1,0:T(8,128)(2,1)S(1)} %bitcast.5, bf16[4,8,1280]{2,1,0:T(8,128)(2,1)S(1)} %copy-done, s32[4,128]{1,0:T(4,128)S(1)} %broadcast_in_dim.8.dest_ref, s32[272]{0:T(512)S(1)} %copy-done.5, f32[32,32]{1,0:T(8,128)S(1)} %copy-done.4, f32[64,32]{1,0:T(8,128)S(1)} %copy-done.3, ...), custom_call_target="tpu_custom_call" | custom-call | tf_op jit(solution)/shard_map/pallas_call | solution.py:448
  39.4 3.1 %copy.10 = bf16[272,4,1024]{2,1,0:T(4,128)(2,1)} copy(bf16[272,4,1024]{2,0,1:T(8,128)(2,1)S(1)} %bitcast.6) | data formatting | bytes 4456448 | tf_op jit(solution)/shard_map/transpose | solution.py:492
Async XLA Ops:
  0.7 2.2 %copy-start = (bf16[4,8,1280]{2,1,0:T(8,128)(2,1)S(1)}, bf16[4,8,1280]{2,1,0:T(8,128)(2,1)}, u32[]{:S(2)}) copy-start(bf16[4,8,1280]{2,1,0:T(8,128)(2,1)} %vis_ref.1) | copy-start | bytes 245764
  0.7 2.2 %copy-start.1 = (f32[128,128]{1,0:T(8,128)S(1)}, f32[128,128]{1,0:T(8,128)}, u32[]{:S(2)}) copy-start(f32[128,128]{1,0:T(8,128)} %constant.11.clone.slot_order_ref) | copy-start | bytes 196612
  0.7 2.2 %copy-start.2 = (f32[64,32]{1,0:T(8,128)S(1)}, f32[64,32]{1,0:T(8,128)}, u32[]{:S(2)}) copy-start(f32[64,32]{1,0:T(8,128)} %constant.10.clone.slot_ref) | copy-start | bytes 24580
  0.7 2.2 %copy-start.3 = (f32[64,32]{1,0:T(8,128)S(1)}, f32[64,32]{1,0:T(8,128)}, u32[]{:S(2)}) copy-start(f32[64,32]{1,0:T(8,128)} %constant.9.clone.pick_ref) | copy-start | bytes 24580
  0.7 2.2 %copy-start.4 = (f32[32,32]{1,0:T(8,128)S(1)}, f32[32,32]{1,0:T(8,128)}, u32[]{:S(2)}) copy-start(f32[32,32]{1,0:T(8,128)} %constant.8.clone.same_ref) | copy-start | bytes 12292
  0.7 2.2 %copy-start.5 = (s32[272]{0:T(512)S(1)}, s32[272]{0:T(512)}, u32[]{:S(2)}) copy-start(s32[272]{0:T(512)} %seg_ref.1) | copy-start | bytes 3268

commit v6 on v5

--- a/solution.py
+++ b/solution.py
@@ -15,7 +15,7 @@
 REACH = 4
 FAR = -(2.0 ** 100)
 OWN = 120
-TOGETHER = 4
+TOGETHER = 2
 LOG2E = math.log2(math.e)
 MESH = pl.DeviceIdType.MESH
 
@@ -60,10 +60,10 @@
     barrier = pltpu.get_barrier_semaphore()
 
     vis_wide = vis_ref[...].astype(jnp.float32)
-    dest_wide = dest_ref[...].astype(jnp.float32)
+    dest_wide = dest_ref[...].reshape(1, vis_count).astype(jnp.float32)
     for shard in range(n_shard):
         listed = [vis_wide[row, shard * groups:(shard + 1) * groups] for row in range(vis_count)]
-        names = [jnp.broadcast_to(dest_wide[row:row + 1], (groups, DH)) for row in range(vis_count)]
+        names = [jnp.broadcast_to(dest_wide[:, row:row + 1], (groups, DH)) for row in range(vis_count)]
         if vis_block > vis_count * groups:
             listed.append(jnp.zeros((vis_block - vis_count * groups, width), jnp.float32))
             names.append(jnp.zeros((vis_block - vis_count * groups, DH), jnp.float32))
@@ -192,6 +192,21 @@
     query_parts = (query_stage, query_listed, query_send, query_recv)
     vis_start(key_parts)
     start(0, own_copies)
+
+    seg_row = seg_ref[...].reshape(1, rows).astype(jnp.float32) + 1.0
+    together = text_mask.shape[2] // half
+    slot_heads = max(1, min(GQ, together * half // slot_count))
+    name = lax.broadcasted_iota(jnp.int32, (DH, rows), 0)
+    at = lax.broadcasted_iota(jnp.int32, (DH, rows), 1)
+    named = jnp.where((name.astype(jnp.float32) + 1.0 == seg_row) | ((name == OWN) & (at < text)), 1.0, 0.0)
+    for part in range(2):
+        narrow = named[:, part * half:(part + 1) * half].astype(jnp.bfloat16)
+        text_mask[part] = jnp.concatenate([narrow] * together, axis=1)
+    slot_mask[...] = jnp.concatenate([named[:, text:]] * slot_heads, axis=1).astype(jnp.bfloat16)
+    ahead = lax.broadcasted_iota(jnp.int32, (half, half), 0) > lax.broadcasted_iota(jnp.int32, (half, half), 1)
+    diagonal[...] = jnp.where(ahead, FAR, 0.0)
+    val_all[DH:, :] = jnp.ones_like(val_all[DH:, :])
+
     vis_wait(key_parts)
 
     block_rows = n_shard * vis_block
@@ -214,7 +229,6 @@
     aux_buf[REACH, 0:aux_rows] = slot_keys.astype(jnp.bfloat16)
     live_col[...] = jnp.broadcast_to(filled[:slot_count], live_col.shape)
     live_across = live_col[...].T[0:1, :]
-    seg_row = seg_ref[...].reshape(1, rows).astype(jnp.float32) + 1.0
     text_tags = seg_row[:, :text]
     slot_tags = jnp.where(live_across > 0, seg_row[:, text:], 0.0)
     tag_rows = jnp.concatenate(
@@ -228,16 +242,16 @@
     )
     aux_buf[REACH, aux_rows:] = tag_rows.astype(jnp.bfloat16)
     start(groups, own_copies)
-    vis_start(query_parts)
-    for item in range(1, groups):
-        start(item, own_copies)
 
     relay_far(0)
     relay_far(groups)
+    vis_start(query_parts)
+    if groups > 1:
+        start(1, own_copies)
     relay_near(0)
     relay_near(groups)
-    if groups > 1:
-        relay_far(1)
+    for item in range(2, groups):
+        start(item, own_copies)
     arrive(groups, 1)
     arrive(groups, 3)
 
@@ -256,18 +270,6 @@
     differs = (name < OWN) & (name.astype(jnp.float32) + 1.0 != tags)
     own_slot = (name == OWN) & (at >= 0) & (at < slot_count)
     key_all[:, DH:] = jnp.where(differs | own_slot, FAR, 0.0).T.astype(jnp.bfloat16)
-    together = text_mask.shape[2] // half
-    slot_heads = max(1, min(GQ, together * half // slot_count))
-    name = lax.broadcasted_iota(jnp.int32, (DH, rows), 0)
-    at = lax.broadcasted_iota(jnp.int32, (DH, rows), 1)
-    named = jnp.where((name.astype(jnp.float32) + 1.0 == seg_row) | ((name == OWN) & (at < text)), 1.0, 0.0)
-    for part in range(2):
-        narrow = named[:, part * half:(part + 1) * half].astype(jnp.bfloat16)
-        text_mask[part] = jnp.concatenate([narrow] * together, axis=1)
-    slot_mask[...] = jnp.concatenate([named[:, text:]] * slot_heads, axis=1).astype(jnp.bfloat16)
-    ahead = lax.broadcasted_iota(jnp.int32, (half, half), 0) > lax.broadcasted_iota(jnp.int32, (half, half), 1)
-    diagonal[...] = jnp.where(ahead, FAR, 0.0)
-    val_all[DH:, :] = jnp.ones_like(val_all[DH:, :])
     scale = LOG2E * DH ** -0.5
 
     def turned(values):
@@ -363,10 +365,10 @@
             low, high = tiles[number][1][:2]
             held, made = score_slots[number % 2], weight_slots[number % 2]
             lanes = state["largest"].shape[1]
-            largest = jnp.max(state["largest"], axis=0, keepdims=True)
+            largest = jnp.max(state["largest"], axis=0, keepdims=True) * scale
 
             def one(at, end):
-                made[at:end, :lanes] = jnp.exp2((held[at:end, :lanes] - largest) * scale).astype(jnp.bfloat16)
+                made[at:end, :lanes] = jnp.exp2(held[at:end, :lanes] * scale - largest).astype(jnp.bfloat16)
 
             count = high - low
             return [functools.partial(one, at, min(at + 64, count)) for at in range(0, count, 64)], lanes
@@ -384,14 +386,14 @@
             step()
         before = None
         for number in range(len(tiles)):
-            if number == len(tiles) // 2:
+            if number == len(tiles) * 4 // 9:
+                @pl.when(group + 1 < groups)
+                def _():
+                    relay_far(group + 1)
+            if number == len(tiles) * 7 // 9:
                 @pl.when(group + 1 < groups)
                 def _():
                     relay_near(group + 1)
-
-                @pl.when(group + 2 < groups)
-                def _():
-                    relay_far(group + 2)
             if before is not None:
                 finish_tile(number - 1, before)
             weigh, lanes = weight_steps(number, state)
@@ -482,7 +484,7 @@
     )(
         text_t,
         vis_rows,
-        jnp.broadcast_to(vis_dest, (vis_count, DH)),
+        vis_dest.reshape(vis_count),
         segments,
         jnp.asarray(same, jnp.float32),
         jnp.asarray(pick, jnp.float32),

time: 42.7 us -> 43.6 us (1.021)
  Pallas kernels: 36.5 us -> 38.1 us
  local copies, waits for them, and re-layouts: 5.95 us -> 5.27 us
    pallas_call x1, Pallas kernels: 36.5 us -> 38.1 us  [shards(): pl.pallas_call(functools.partial(kernel, n_group, n_seq, n_shard), out_sh...]
    broadcast_in_dim x1 -> x0, local copies, waits for them, and re-layouts: 0.72 us -> none  [shards(): jnp.broadcast_to(vis_dest, (vis_count, DH))]
    unnamed x13 -> x15, local copies, waits for them, and re-layouts: 2.14 us -> 2.19 us
where the time goes in v6:
time: 43.6 us; the launch traced here: 43.5 us
  Pallas kernels  38.1 us (87%)
  local copies, waits for them, and re-layouts  5.27 us (12%)
    pallas_call x1, Pallas kernels, shards(): pl.pallas_call(functools.partial(kernel, n_group, n_seq, n_shard), out_sh...  38.1 us
    transpose x1, local copies, waits for them, and re-layouts, shards(): return result.transpose(1, 0, 2)  3.08 us
    unnamed x15, local copies, waits for them, and re-layouts  2.19 us

profile of v6, /device:TPU:9, one launch (start us, length us, event | category | flops | bytes accessed | tf_op | source)
XLA Modules:
  0.0 43.5 jit_solution(2089805946451190091)
XLA Ops:
  0.0 0.0 copy-start
  0.0 0.0 copy-start.1
  0.0 0.0 copy-start.2
  0.0 0.0 copy-start.3
  0.0 0.0 copy-start.4
  0.0 0.0 copy-start.5
  0.0 0.0 copy-start.6
  0.1 2.2 %copy.12 = bf16[256,4,1280]{2,0,1:T(8,128)(2,1)S(1)} copy(bf16[256,4,1280]{2,1,0:T(4,128)(2,1)} %param.8) | data formatting | bytes 5242880 | tf_op args[0]
  2.2 0.0 copy-done
  2.2 0.0 copy-done.1
  2.2 0.0 copy-done.2
  2.2 0.0 copy-done.3
  2.3 0.0 copy-done.4
  2.3 0.0 copy-done.5
  2.3 0.0 copy-done.6
  2.3 38.1 %shard_map.82 = bf16[4,272,1024]{2,1,0:T(8,128)(2,1)S(1)} custom-call(bf16[4,256,1280]{2,1,0:T(8,128)(2,1)S(1)} %bitcast.5, bf16[4,8,1280]{2,1,0:T(8,128)(2,1)S(1)} %copy-done, s32[4]{0:T(128)S(1)} %bitcast.7, s32[272]{0:T(512)S(1)} %copy-done.5, f32[32,32]{1,0:T(8,128)S(1)} %copy-done.4, f32[64,32]{1,0:T(8,128)S(1)} %copy-done.3, f32[64,32]{1,0:T(8,128)S(1)} %copy-done.2, ...), custom_call_target="tpu_custom_call" | custom-call | tf_op jit(solution)/shard_map/pallas_call | solution.py:450
  40.4 3.1 %copy.10 = bf16[272,4,1024]{2,1,0:T(4,128)(2,1)} copy(bf16[272,4,1024]{2,0,1:T(8,128)(2,1)S(1)} %bitcast.6) | data formatting | bytes 4456448 | tf_op jit(solution)/shard_map/transpose | solution.py:494
Async XLA Ops:
  0.0 2.2 %copy-start = (bf16[4,8,1280]{2,1,0:T(8,128)(2,1)S(1)}, bf16[4,8,1280]{2,1,0:T(8,128)(2,1)}, u32[]{:S(2)}) copy-start(bf16[4,8,1280]{2,1,0:T(8,128)(2,1)} %vis_ref.1) | copy-start | bytes 245764
  0.0 2.2 %copy-start.1 = (f32[128,128]{1,0:T(8,128)S(1)}, f32[128,128]{1,0:T(8,128)}, u32[]{:S(2)}) copy-start(f32[128,128]{1,0:T(8,128)} %constant.11.clone.slot_order_ref) | copy-start | bytes 196612
  0.0 2.2 %copy-start.2 = (f32[64,32]{1,0:T(8,128)S(1)}, f32[64,32]{1,0:T(8,128)}, u32[]{:S(2)}) copy-start(f32[64,32]{1,0:T(8,128)} %constant.10.clone.slot_ref) | copy-start | bytes 24580
  0.0 2.2 %copy-start.3 = (f32[64,32]{1,0:T(8,128)S(1)}, f32[64,32]{1,0:T(8,128)}, u32[]{:S(2)}) copy-start(f32[64,32]{1,0:T(8,128)} %constant.9.clone.pick_ref) | copy-start | bytes 24580
  0.0 2.2 %copy-start.4 = (f32[32,32]{1,0:T(8,128)S(1)}, f32[32,32]{1,0:T(8,128)}, u32[]{:S(2)}) copy-start(f32[32,32]{1,0:T(8,128)} %constant.8.clone.same_ref) | copy-start | bytes 12292
  0.0 2.2 %copy-start.5 = (s32[272]{0:T(512)S(1)}, s32[272]{0:T(512)}, u32[]{:S(2)}) copy-start(s32[272]{0:T(512)} %seg_ref.1) | copy-start | bytes 3268
  0.0 2.2 %copy-start.6 = (s32[4,1]{0,1:T(1,128)S(1)}, s32[4,1]{0,1:T(1,128)}, u32[]{:S(2)}) copy-start(s32[4,1]{0,1:T(1,128)} %param.10) | copy-start | bytes 52

commit v7 on v6

--- a/solution.py
+++ b/solution.py
@@ -242,16 +242,16 @@
     )
     aux_buf[REACH, aux_rows:] = tag_rows.astype(jnp.bfloat16)
     start(groups, own_copies)
+    vis_start(query_parts)
+    for item in range(1, groups):
+        start(item, own_copies)
 
     relay_far(0)
     relay_far(groups)
-    vis_start(query_parts)
-    if groups > 1:
-        start(1, own_copies)
     relay_near(0)
     relay_near(groups)
-    for item in range(2, groups):
-        start(item, own_copies)
+    if groups > 1:
+        relay_far(1)
     arrive(groups, 1)
     arrive(groups, 3)
 
@@ -365,10 +365,10 @@
             low, high = tiles[number][1][:2]
             held, made = score_slots[number % 2], weight_slots[number % 2]
             lanes = state["largest"].shape[1]
-            largest = jnp.max(state["largest"], axis=0, keepdims=True) * scale
+            largest = jnp.max(state["largest"], axis=0, keepdims=True)
 
             def one(at, end):
-                made[at:end, :lanes] = jnp.exp2(held[at:end, :lanes] * scale - largest).astype(jnp.bfloat16)
+                made[at:end, :lanes] = jnp.exp2((held[at:end, :lanes] - largest) * scale).astype(jnp.bfloat16)
 
             count = high - low
             return [functools.partial(one, at, min(at + 64, count)) for at in range(0, count, 64)], lanes
@@ -386,14 +386,14 @@
             step()
         before = None
         for number in range(len(tiles)):
-            if number == len(tiles) * 4 // 9:
-                @pl.when(group + 1 < groups)
-                def _():
-                    relay_far(group + 1)
-            if number == len(tiles) * 7 // 9:
+            if number == len(tiles) // 2:
                 @pl.when(group + 1 < groups)
                 def _():
                     relay_near(group + 1)
+
+                @pl.when(group + 2 < groups)
+                def _():
+                    relay_far(group + 2)
             if before is not None:
                 finish_tile(number - 1, before)
             weigh, lanes = weight_steps(number, state)

time: 43.6 us -> 41.8 us (0.959)
  Pallas kernels: 38.1 us -> 36.3 us
    pallas_call x1, Pallas kernels: 38.1 us -> 36.3 us  [shards(): pl.pallas_call(functools.partial(kernel, n_group, n_seq, n_shard), out_sh...]
where the time goes in v7:
time: 41.8 us; the launch traced here: 41.6 us
  Pallas kernels  36.3 us (87%)
  local copies, waits for them, and re-layouts  5.27 us (13%)
    pallas_call x1, Pallas kernels, shards(): pl.pallas_call(functools.partial(kernel, n_group, n_seq, n_shard), out_sh...  36.3 us
    transpose x1, local copies, waits for them, and re-layouts, shards(): return result.transpose(1, 0, 2)  3.08 us
    unnamed x15, local copies, waits for them, and re-layouts  2.19 us

profile of v7, /device:TPU:9, one launch (start us, length us, event | category | flops | bytes accessed | tf_op | source)
XLA Modules:
  0.0 41.6 jit_solution(4583283518591951911)
XLA Ops:
  0.0 0.0 copy-start
  0.0 0.0 copy-start.1
  0.0 0.0 copy-start.2
  0.0 0.0 copy-start.3
  0.0 0.0 copy-start.4
  0.0 0.0 copy-start.5
  0.0 0.0 copy-start.6
  0.1 2.2 %copy.12 = bf16[256,4,1280]{2,0,1:T(8,128)(2,1)S(1)} copy(bf16[256,4,1280]{2,1,0:T(4,128)(2,1)} %param.8) | data formatting | bytes 5242880 | tf_op args[0]
  2.2 0.0 copy-done
  2.2 0.0 copy-done.1
  2.2 0.0 copy-done.2
  2.2 0.0 copy-done.3
  2.3 0.0 copy-done.4
  2.3 0.0 copy-done.5
  2.3 0.0 copy-done.6
  2.3 36.3 %shard_map.82 = bf16[4,272,1024]{2,1,0:T(8,128)(2,1)S(1)} custom-call(bf16[4,256,1280]{2,1,0:T(8,128)(2,1)S(1)} %bitcast.5, bf16[4,8,1280]{2,1,0:T(8,128)(2,1)S(1)} %copy-done, s32[4]{0:T(128)S(1)} %bitcast.7, s32[272]{0:T(512)S(1)} %copy-done.5, f32[32,32]{1,0:T(8,128)S(1)} %copy-done.4, f32[64,32]{1,0:T(8,128)S(1)} %copy-done.3, f32[64,32]{1,0:T(8,128)S(1)} %copy-done.2, ...), custom_call_target="tpu_custom_call" | custom-call | tf_op jit(solution)/shard_map/pallas_call | solution.py:450
  38.6 3.1 %copy.10 = bf16[272,4,1024]{2,1,0:T(4,128)(2,1)} copy(bf16[272,4,1024]{2,0,1:T(8,128)(2,1)S(1)} %bitcast.6) | data formatting | bytes 4456448 | tf_op jit(solution)/shard_map/transpose | solution.py:494
Async XLA Ops:
  0.0 2.2 %copy-start = (bf16[4,8,1280]{2,1,0:T(8,128)(2,1)S(1)}, bf16[4,8,1280]{2,1,0:T(8,128)(2,1)}, u32[]{:S(2)}) copy-start(bf16[4,8,1280]{2,1,0:T(8,128)(2,1)} %vis_ref.1) | copy-start | bytes 245764
  0.0 2.2 %copy-start.1 = (f32[128,128]{1,0:T(8,128)S(1)}, f32[128,128]{1,0:T(8,128)}, u32[]{:S(2)}) copy-start(f32[128,128]{1,0:T(8,128)} %constant.11.clone.slot_order_ref) | copy-start | bytes 196612
  0.0 2.2 %copy-start.2 = (f32[64,32]{1,0:T(8,128)S(1)}, f32[64,32]{1,0:T(8,128)}, u32[]{:S(2)}) copy-start(f32[64,32]{1,0:T(8,128)} %constant.10.clone.slot_ref) | copy-start | bytes 24580
  0.0 2.2 %copy-start.3 = (f32[64,32]{1,0:T(8,128)S(1)}, f32[64,32]{1,0:T(8,128)}, u32[]{:S(2)}) copy-start(f32[64,32]{1,0:T(8,128)} %constant.9.clone.pick_ref) | copy-start | bytes 24580
  0.0 2.2 %copy-start.4 = (f32[32,32]{1,0:T(8,128)S(1)}, f32[32,32]{1,0:T(8,128)}, u32[]{:S(2)}) copy-start(f32[32,32]{1,0:T(8,128)} %constant.8.clone.same_ref) | copy-start | bytes 12292
  0.0 2.2 %copy-start.5 = (s32[272]{0:T(512)S(1)}, s32[272]{0:T(512)}, u32[]{:S(2)}) copy-start(s32[272]{0:T(512)} %seg_ref.1) | copy-start | bytes 3268
  0.0 2.2 %copy-start.6 = (s32[4,1]{0,1:T(1,128)S(1)}, s32[4,1]{0,1:T(1,128)}, u32[]{:S(2)}) copy-start(s32[4,1]{0,1:T(1,128)} %param.10) | copy-start | bytes 52
